TPU v7x, 32 devices: a whole 2x2x4 slice. The times are simulated.
32 devices in a mesh: blk: 16 (over z, y, core), tensor: 2 (over x).
Axes of the slice: x: 2, y: 2, z: 4, core: 2. Of those that a mesh axis runs over, the one named last changes fastest.
Arguments:
- activations: bfloat16 [6144, 5120], P('blk'), may hold values from -6 to 6
- out_grad: bfloat16 [6144, 5120], P('blk'), may hold values from -12 to 12
- gate_weight: bfloat16 [16, 5120, 108], P('blk', None, 'tensor'), may hold values from -0.078125 to 0.078125
- up_weight: bfloat16 [16, 5120, 108], P('blk', None, 'tensor'), may hold values from -0.078125 to 0.078125
- down_weight: bfloat16 [16, 108, 5120], P('blk', 'tensor'), may hold values from -0.625 to 0.625
Outputs:
- in_grad: bfloat16 [6144, 5120], P(('blk', 'tensor'))
- gate_accum: float32 [16, 5120, 108], P('blk', None, 'tensor')
- up_accum: float32 [16, 5120, 108], P('blk', None, 'tensor')
- down_accum: float32 [16, 108, 5120], P('blk', 'tensor')
All inputs are finite; a program needn't handle non-finite values.
Results may differ from a plain program's by a relative error of at most 0.006.
Values may be sent and summed in bfloat16 or wider, within the bound.
No kernel may reach another device: no remote copies, remote signals or barrier semaphores. Data moves between devices by JAX's collectives and lax.ppermute only.
A program may use at most 128 MiB of HBM per device.

v0:
```python
import functools

import jax
import jax.numpy as jnp
from jax import lax
from jax.experimental import pallas as pl
from jax.experimental.pallas import tpu as pltpu
from jax.sharding import PartitionSpec as P

F32 = jnp.float32
BF16 = jnp.bfloat16
VMEM_LIMIT = 16 * 2**20
VMEM = pl.BlockSpec(memory_space=pltpu.VMEM)
ANY = pl.BlockSpec(memory_space=pl.ANY)
HBM = pl.BlockSpec(memory_space=pltpu.HBM)
SMEM = pl.BlockSpec(memory_space=pltpu.SMEM)


def from_behind(value, axis, by):
    devices = lax.axis_size(axis)
    return lax.ppermute(value, axis, [(i, (i + by) % devices) for i in range(devices)])


def column_block(width, limit):
    block = limit
    while width % block:
        block -= 128
    return block


def columns(width, limit=1280):
    block = column_block(width, limit)
    return [pl.ds(at, block) for at in range(0, width, block)]


def in_vmem(*arrays):
    return [pltpu.with_memory_space_constraint(a, pltpu.VMEM) for a in arrays]


def params(flops, nbytes):
    return dict(
        compiler_params=pltpu.CompilerParams(vmem_limit_bytes=VMEM_LIMIT),
        cost_estimate=pl.CostEstimate(flops=flops, bytes_accessed=nbytes, transcendentals=0),
    )


def stacked(gate, up, step):
    if gate.shape[0] == step:
        return jnp.concatenate([gate, up], axis=0)
    pad = jnp.zeros((step - gate.shape[0], gate.shape[1]), gate.dtype)
    return jnp.concatenate([gate, pad, up, pad], axis=0)


def pre_of(stack_ref, gate_ref, up_ref, rows_ref):
    total = None
    for at in columns(stack_ref.shape[1]):
        weight = stacked(gate_ref[:, at], up_ref[:, at], stack_ref.shape[0] // 2)
        stack_ref[:, at] = weight
        term = lax.dot_general(
            weight, rows_ref[:, at], (((1,), (1,)), ((), ())), preferred_element_type=F32
        )
        total = term if total is None else total + term
    return total


def hidden_of(pre):
    step = pre.shape[0] // 2
    gate_pre, up_pre = pre[:step], pre[step:]
    return (gate_pre * jax.nn.sigmoid(gate_pre) * up_pre).astype(BF16)


def product(weight_ref, rows_ref):
    total = None
    for at in columns(weight_ref.shape[1]):
        term = lax.dot_general(
            weight_ref[:, at], rows_ref[:, at], (((1,), (1,)), ((), ())), preferred_element_type=F32
        )
        total = term if total is None else total + term
    return total


def grads_of(pre, grad_hidden):
    step, hidden = pre.shape[0] // 2, grad_hidden.shape[0]
    if step > hidden:
        pad = jnp.zeros((step - hidden, grad_hidden.shape[1]), F32)
        grad_hidden = jnp.concatenate([grad_hidden, pad], axis=0)
    gate_pre, up_pre = pre[:step], pre[step:]
    sigmoid_part = jax.nn.sigmoid(gate_pre)
    slope_part = sigmoid_part * (1.0 + gate_pre * (1.0 - sigmoid_part))
    grad_gate = (grad_hidden * up_pre * slope_part).astype(BF16)
    grad_up = (grad_hidden * (gate_pre * sigmoid_part)).astype(BF16)
    return jnp.concatenate([grad_gate, grad_up], axis=0)


def terms_of(early_ref, late_ref, hidden, grads, x_ref, g_ref):
    step = hidden.shape[0]
    for at in columns(x_ref.shape[1]):
        down = jnp.dot(hidden, g_ref[:, at], preferred_element_type=F32)
        gate_up = jnp.dot(grads, x_ref[:, at], preferred_element_type=F32)
        early = jnp.concatenate([down, gate_up[:step]], axis=0)
        early_ref[:, at] = early.astype(early_ref.dtype)
        late_ref[:, at] = gate_up[step:].astype(late_ref.dtype)


def own_kernel(x_ref, g_ref, gate_in, up_in, down_in, stack_ref, grads_ref, hidden_ref, gate_ref, up_ref, down_ref, sem):
    copies = [
        pltpu.make_async_copy(source, into, sem.at[n])
        for n, (source, into) in enumerate(
            [(gate_in, gate_ref), (up_in, up_ref), (down_in, down_ref)]
        )
    ]
    for copy in copies:
        copy.start()
    copies[0].wait()
    copies[1].wait()
    pre = pre_of(stack_ref, gate_ref, up_ref, x_ref)
    hidden_ref[...] = hidden_of(pre)
    copies[2].wait()
    grads_ref[...] = grads_of(pre, product(down_ref, g_ref))


def own_meeting(x, g, w_gate, w_up, w_down, step):
    rows, width = x.shape
    weights = [pltpu.with_memory_space_constraint(w, pltpu.HBM) for w in (w_gate, w_up, w_down)]
    return pl.pallas_call(
        own_kernel,
        in_specs=[VMEM] * 2 + [HBM] * 3,
        out_specs=[VMEM] * 3,
        out_shape=[
            pltpu.VMEM((2 * step, width), BF16),
            pltpu.VMEM((2 * step, rows), BF16),
            pltpu.VMEM((step, rows), BF16),
        ],
        scratch_shapes=[pltpu.VMEM(w_gate.shape, BF16)] * 3 + [pltpu.SemaphoreType.DMA((3,))],
        name="own_meeting",
        **params(6 * step * rows * width, 4 * rows * width),
    )(*in_vmem(x, g), *weights)


def grad_hidden_kernel(g_ref, down_ref, after_ref, out_ref):
    del after_ref
    out_ref[...] = product(down_ref, g_ref)


def grad_hidden_of(g, w_down, after):
    rows, width = g.shape
    return pl.pallas_call(
        grad_hidden_kernel,
        in_specs=[VMEM] * 2 + [ANY],
        out_specs=VMEM,
        out_shape=pltpu.VMEM((w_down.shape[0], rows), F32),
        name="grad_hidden",
        **params(2 * w_down.size * rows, 2 * g.size),
    )(*in_vmem(g, w_down), after)


def second_kernel(n_stacks, halves, x_ref, g_ref, prev_ref, own_ref, index_ref, *refs):
    weights, (early_ref, late_ref, *refs) = refs[: 2 * n_stacks], refs[2 * n_stacks :]
    stack_refs, grads_refs = refs[:n_stacks], refs[n_stacks:]
    step = late_ref.shape[0]
    pre = pre_of(stack_refs[0], weights[0], weights[1], x_ref)
    grads = grads_of(pre, prev_ref[...])
    terms_of(early_ref, late_ref, hidden_of(pre), grads, x_ref, g_ref)
    both = jnp.concatenate([own_ref[...], grads], axis=0)
    if halves == 1:
        grads_refs[0][...] = both
        return
    half = both.shape[1] // 2

    @pl.when(index_ref[0] == 0)
    def _():
        grads_refs[0][...] = both[:, :half]
        grads_refs[1][...] = both[:, half:]

    @pl.when(index_ref[0] != 0)
    def _():
        grads_refs[0][...] = both[:, half:]
        grads_refs[1][...] = both[:, :half]

    for n in range(1, n_stacks):
        for at in columns(x_ref.shape[1]):
            gate, up = weights[2 * n][:, at], weights[2 * n + 1][:, at]
            stack_refs[n][:, at] = stacked(gate, up, step)


def second_meeting(x, g, grad_hidden, own_grads, weights, index, halves):
    rows, width = x.shape
    step2 = own_grads.shape[0]
    n_stacks = len(weights) // 2
    return pl.pallas_call(
        functools.partial(second_kernel, n_stacks, halves),
        in_specs=[VMEM] * 4 + [SMEM] + [VMEM] * len(weights),
        out_specs=[VMEM] * (2 + n_stacks + halves),
        out_shape=[pltpu.VMEM((step2, width), BF16), pltpu.VMEM((step2 // 2, width), BF16)]
        + [pltpu.VMEM((step2, width), BF16)] * n_stacks
        + [pltpu.VMEM((2 * step2, rows // halves), BF16)] * halves,
        name="second_meeting",
        **params(6 * step2 * rows * width, 4 * rows * width),
    )(*in_vmem(x, g, grad_hidden, own_grads), index.reshape(1), *in_vmem(*weights))


def stack_kernel(gate_ref, up_ref, after_ref, out_ref):
    del after_ref
    for at in columns(out_ref.shape[1]):
        out_ref[:, at] = stacked(gate_ref[:, at], up_ref[:, at], out_ref.shape[0] // 2)


def stack(w_gate, w_up, step, after):
    width = w_gate.shape[1]
    return pl.pallas_call(
        stack_kernel,
        in_specs=[VMEM, VMEM, ANY],
        out_specs=VMEM,
        out_shape=pltpu.VMEM((2 * step, width), BF16),
        name="stack",
        **params(0, 8 * step * width),
    )(*in_vmem(w_gate, w_up), after)


def sums_kernel(x_ref, g_ref, hidden_ref, grads_ref, after_ref, early_ref, late_ref):
    del after_ref
    terms_of(early_ref, late_ref, hidden_ref[...], grads_ref[...], x_ref, g_ref)


def own_sums(x, g, hidden, grads, after):
    rows, width = x.shape
    return pl.pallas_call(
        sums_kernel,
        in_specs=[VMEM] * 4 + [ANY],
        out_specs=[VMEM] * 2,
        out_shape=[pltpu.VMEM((n * hidden.shape[0], width), F32) for n in (2, 1)],
        name="own_sums",
        **params(6 * hidden.shape[0] * rows * width, 4 * rows * width),
    )(*in_vmem(x, g, hidden, grads), after)


def total_kernel(own_in, back_in, after_ref, *refs):
    del after_ref
    out_refs, (own_ref, back_ref, in_sem, out_sem) = refs[:-4], refs[-4:]
    step, hidden = own_ref.shape[0] // len(out_refs), out_refs[0].shape[0]
    rows = [pl.ds(k * step, step) for k in range(len(out_refs))]
    loads = [pltpu.make_async_copy(back_in, back_ref, in_sem.at[0])] + [
        pltpu.make_async_copy(own_in.at[at, :], own_ref.at[at, :], in_sem.at[1 + k])
        for k, at in enumerate(rows)
    ]
    for copy in loads:
        copy.start()
    loads[0].wait()
    stores = []
    for k, at in enumerate(rows):
        loads[1 + k].wait()
        for first in range(0, step, 8):
            part = pl.ds(k * step + first, 8)
            own_ref[part, :] = own_ref[part, :] + back_ref[part, :].astype(F32)
            for r in range(first, min(first + 8, hidden)):
                row = own_ref.at[pl.ds(k * step + r, 1), :]
                stores.append(pltpu.make_async_copy(row, out_refs[k].at[r], out_sem.at[k, r]))
                stores[-1].start()
    for copy in stores:
        copy.wait()


def totals(own, back, count, hidden, after):
    rows, width = own.shape
    return pl.pallas_call(
        total_kernel,
        in_specs=[ANY] * 3,
        out_specs=[HBM] * count,
        out_shape=[jax.ShapeDtypeStruct((hidden, 1, width), F32)] * count,
        scratch_shapes=[
            pltpu.VMEM((rows, width), F32),
            pltpu.VMEM((rows, width), BF16),
            pltpu.SemaphoreType.DMA((1 + count,)),
            pltpu.SemaphoreType.DMA((count, hidden)),
        ],
        name="totals",
        **params(rows * width, 10 * rows * width),
    )(own, back, after)


def in_grad_kernel(left_counts, right_counts, after_ref, *refs):
    del after_ref
    *refs, out_ref, scratch, sem = refs
    stores = []
    for n, at in enumerate(columns(out_ref.shape[1])):
        rest = list(refs)
        result = None
        for n_left, groups in zip(left_counts, right_counts):
            left = [rest.pop(0)[...] for _ in range(n_left)]
            right = []
            for count in groups:
                term = rest.pop(0)[:, at]
                for _ in range(count - 1):
                    term = term + rest.pop(0)[:, at]
                right.append(term)
            partial = lax.dot_general(
                jnp.concatenate(left, axis=0),
                jnp.concatenate(right, axis=0),
                (((0,), (0,)), ((), ())),
                preferred_element_type=F32,
            )
            partial = partial.astype(BF16).astype(F32)
            result = partial if result is None else result + partial
        scratch[:, at] = result.astype(BF16)
        stores.append(pltpu.make_async_copy(scratch.at[:, at], out_ref.at[:, at], sem.at[n]))
        stores[-1].start()
    for copy in stores:
        copy.wait()


def in_grad_of(after, *partials):
    operands = []
    for lefts, rights in partials:
        operands += lefts + [t for r in rights for t in r]
    rows, width = partials[0][0][0].shape[1], partials[0][1][0][0].shape[1]
    return pl.pallas_call(
        functools.partial(
            in_grad_kernel,
            [len(l) for l, _ in partials],
            [[len(t) for t in r] for _, r in partials],
        ),
        in_specs=[ANY] + [VMEM] * len(operands),
        out_specs=HBM,
        out_shape=jax.ShapeDtypeStruct((rows, width), BF16),
        scratch_shapes=[
            pltpu.VMEM((rows, width), BF16),
            pltpu.SemaphoreType.DMA((len(columns(width)),)),
        ],
        name="in_grad",
        **params(
            2 * sum(t.shape[0] for l, _ in partials for t in l) * rows * width,
            2 * sum(t.size for t in operands) + 2 * rows * width,
        ),
    )(after, *in_vmem(*operands))


def local(activations, out_grad, gate_weight, up_weight, down_weight):
    n_blk, n_tensor = lax.axis_size("blk"), lax.axis_size("tensor")
    hidden = gate_weight.shape[2]
    step = -(-hidden // 8) * 8
    pairs = n_tensor == 2 and n_blk % 2 == 0
    w_gate, w_up, w_down = gate_weight[0].T, up_weight[0].T, down_weight[0]
    prev_down, prev_gate, prev_up = [from_behind(w, "blk", 1) for w in (w_down, w_gate, w_up)]
    weights = [prev_gate, prev_up]
    if pairs:
        axes = ("blk", "tensor")
        swap = [(0, 1), (1, 0)]
        on_chip = [(2 * b + j, 2 * (b + 1) + j) for b in range(0, n_blk, 2) for j in range(2)]
        across = [(2 * b + j, 2 * b + 1 - j) for b in range(0, n_blk, 2) for j in range(2)]
        other_gate, other_up = [lax.ppermute(w, "tensor", swap) for w in (w_gate, w_up)]

    w_gu, own_grads, own_hidden = own_meeting(activations, out_grad, w_gate, w_up, w_down, step)
    grad_hidden = grad_hidden_of(out_grad, prev_down, own_grads)
    early, late, prev_gu, *grads = second_meeting(
        activations,
        out_grad,
        grad_hidden,
        own_grads,
        weights,
        lax.axis_index("tensor"),
        2 if pairs else 1,
    )
    back_early, back_late = [from_behind(t, "blk", -1) for t in (early, late)]
    sums_early, sums_late = own_sums(activations, out_grad, own_hidden, own_grads, prev_gu)
    total_down, total_gate = totals(sums_early, back_early, 2, hidden, prev_gu)
    if pairs:
        mine, sent = grads
        prev_other_even = lax.ppermute(prev_gu, axes, across)
        theirs = lax.ppermute(sent, "tensor", swap)
        other_gu = stack(other_gate, other_up, step, theirs)
        prev_other_odd = lax.ppermute(other_gu, axes, on_chip)
        in_grad = in_grad_of(
            total_gate,
            ([mine], [[w_gu], [prev_gu]]),
            ([theirs], [[other_gu], [prev_other_even, prev_other_odd]]),
        )
        after = in_grad
    else:
        after = in_grad_of(prev_gu, (grads, [[w_gu], [prev_gu]]))
        in_grad = lax.psum_scatter(after, "tensor", scatter_dimension=0, tiled=True)
    [total_up] = totals(sums_late, back_late, 1, hidden, after)
    return (
        in_grad,
        total_gate.transpose(1, 2, 0),
        total_up.transpose(1, 2, 0),
        total_down.transpose(1, 0, 2),
    )


def solution(mesh):
    in_specs = (
        P("blk", None),
        P("blk", None),
        P("blk", None, "tensor"),
        P("blk", None, "tensor"),
        P("blk", "tensor", None),
    )
    out_specs = (
        P(("blk", "tensor"), None),
        P("blk", None, "tensor"),
        P("blk", None, "tensor"),
        P("blk", "tensor", None),
    )
    return jax.shard_map(local, mesh=mesh, in_specs=in_specs, out_specs=out_specs, check_vma=False)
```

profile of v0, /device:TPU:0, one launch (start us, length us, event | category | flops | bytes accessed | tf_op | source)
XLA Modules:
  0.0 55.8 jit_solution(16078295950430736392)
XLA Ops:
  0.6 0.5 collective-permute-start
  1.1 2.6 %collective-permute-start.1 = (bf16[54,5120]{1,0:T(8,128)(2,1)}, bf16[54,5120]{1,0:T(8,128)(2,1)S(1)}, u32[]{:S(2)}, u32[]{:S(2)}) collective-permute-start(bf16[54,5120]{1,0:T(8,128)(2,1)} %bitcast.15), channel_id=1, source_target_pairs={{0,2},{2,4},{4,6},{6,8},{8,10},{10,12},{12,14},{14,16},{16,18},{18... | collective-permute-start | bytes 1658888 | tf_op jit(solution)/shard_map/ppermute | solution.py:21
  3.8 0.1 collective-permute-start.2
  3.8 1.5 %collective-permute-start.5 = (bf16[54,5120]{1,0:T(8,128)(2,1)}, bf16[54,5120]{1,0:T(8,128)(2,1)S(1)}, u32[]{:S(2)}, u32[]{:S(2)}) collective-permute-start(bf16[54,5120]{1,0:T(8,128)(2,1)} %bitcast.16), channel_id=1, source_target_pairs={{0,1},{1,0},{2,3},{3,2},{4,5},{5,4},{6,7},{7,6},{8,9},{9,8},{10,11... | collective-permute-start | bytes 1658888 | tf_op jit(solution)/shard_map/ppermute | solution.py:350
  5.3 0.5 collective-permute-start.6
  5.9 0.0 copy-start
  5.9 2.1 %copy-done = bf16[384,5120]{1,0:T(8,128)(2,1)S(1)} copy-done((bf16[384,5120]{1,0:T(8,128)(2,1)S(1)}, bf16[384,5120]{1,0:T(8,128)(2,1)}, u32[]{:S(2)}) %copy-start) | copy-done | bytes 3932184
  8.0 0.0 copy-start.2
  8.0 2.1 %copy-done.2 = bf16[384,5120]{1,0:T(8,128)(2,1)S(1)} copy-done((bf16[384,5120]{1,0:T(8,128)(2,1)S(1)}, bf16[384,5120]{1,0:T(8,128)(2,1)}, u32[]{:S(2)}) %copy-start.2) | copy-done | bytes 3932184
  10.1 0.0 copy-start.1
  10.1 4.6 %own_meeting.1 = (bf16[112,5120]{1,0:T(8,128)(2,1)S(1)}, bf16[112,384]{1,0:T(8,128)(2,1)S(1)}, bf16[56,384]{1,0:T(8,128)(2,1)S(1)}) custom-call(bf16[384,5120]{1,0:T(8,128)(2,1)S(1)} %copy-done.2, bf16[384,5120]{1,0:T(8,128)(2,1)S(1)} %copy-done, bf16[54,5120]{1,0:T(8,128)(2,1)} %bitcast.17, bf16[54,5120]{1,0:T(8,128)(2,1)} %bitcast.20, ...), custom_call_target="tpu_custom_call" | custom-call | flops 660602880 | bytes 7864320 | tf_op jit(solution)/shard_map/own_meeting/pallas_call | solution.py:125
  14.7 0.0 collective-permute-done.down_ref
  14.7 0.0 copy-done.1
  14.7 1.3 %grad_hidden.1.prev_ref = f32[54,384]{1,0:T(8,128)S(1)} custom-call(bf16[384,5120]{1,0:T(8,128)(2,1)S(1)} %copy-done.1, bf16[54,5120]{1,0:T(8,128)(2,1)S(1)} %collective-permute-done.down_ref, bf16[112,384]{1,0:T(8,128)(2,1)S(1)} %get-tuple-element.17.after_ref.own_ref.grads_ref), custom_call_target="tpu_custom_call" | custom-call | flops 212336640 | bytes 3932160 | tf_op jit(solution)/shard_map/grad_hidden/pallas_call | solution.py:147
  16.0 3.9 %collective-permute-done.1.refs_0_ = bf16[54,5120]{1,0:T(8,128)(2,1)S(1)} collective-permute-done((bf16[54,5120]{1,0:T(8,128)(2,1)}, bf16[54,5120]{1,0:T(8,128)(2,1)S(1)}, u32[]{:S(2)}, u32[]{:S(2)}) %collective-permute-start.1) | collective-permute-done | bytes 552992 | tf_op jit(solution)/shard_map/ppermute | solution.py:21
  19.9 6.1 %collective-permute-done.2.refs_1_ = bf16[54,5120]{1,0:T(8,128)(2,1)S(1)} collective-permute-done((bf16[54,5120]{1,0:T(8,128)(2,1)}, bf16[54,5120]{1,0:T(8,128)(2,1)S(1)}, u32[]{:S(2)}, u32[]{:S(2)}) %collective-permute-start.2) | collective-permute-done | bytes 552992 | tf_op jit(solution)/shard_map/ppermute | solution.py:21
  26.0 0.0 copy-start.3
  26.0 3.3 %second_meeting.1 = (bf16[112,5120]{1,0:T(8,128)(2,1)S(1)}, bf16[56,5120]{1,0:T(8,128)(2,1)S(1)}, bf16[112,5120]{1,0:T(8,128)(2,1)S(1)}, bf16[224,192]{1,0:T(8,128)(2,1)S(1)}, bf16[224,192]{1,0:T(8,128)(2,1)S(1)}) custom-call(bf16[384,5120]{1,0:T(8,128)(2,1)S(1)} %copy-done.2, bf16[384,5120]{1,0:T(8,128)(2,1)S(1)} %copy-done.1, ...), custom_call_target="tpu_custom_call" | custom-call | flops 1321205760 | bytes 7864320 | tf_op jit(solution)/shard_map/second_meeting/pallas_call | solution.py:190
  29.4 2.0 %collective-permute-start.4 = (bf16[224,192]{1,0:T(8,128)(2,1)S(1)}, bf16[224,192]{1,0:T(8,128)(2,1)S(1)}, u32[]{:S(2)}, u32[]{:S(2)}) collective-permute-start(bf16[224,192]{1,0:T(8,128)(2,1)S(1)} %get-tuple-element.24), channel_id=1, source_target_pairs={{0,1},{1,0},{2,3},{3,2},{4,5},{5,4},{6,7},{7,6},{8,9},{9,8},{10,11... | collective-permute-start | bytes 258056 | tf_op jit(solution)/shard_map/ppermute | solution.py:369
  31.4 0.0 collective-permute-start.3
  31.4 2.0 %collective-permute-start.7 = (bf16[112,5120]{1,0:T(8,128)(2,1)S(1)}, bf16[112,5120]{1,0:T(8,128)(2,1)S(1)}, u32[]{:S(2)}, u32[]{:S(2)}) collective-permute-start(bf16[112,5120]{1,0:T(8,128)(2,1)S(1)} %get-tuple-element.18.after_ref.refs_2_), channel_id=1, source_target_pairs={{0,1},{1,0},{4,5},{5,4},{8,9},{9,8},{12,13},{13,12},{16,17},{17,16... | collective-permute-start | bytes 3440648 | tf_op jit(solution)/shard_map/ppermute | solution.py:368
  33.4 0.0 collective-permute-done.5.gate_ref
  33.4 0.0 collective-permute-done.6.up_ref
  33.4 1.2 %collective-permute-done.4.after_ref.refs_3_ = bf16[224,192]{1,0:T(8,128)(2,1)S(1)} collective-permute-done((bf16[224,192]{1,0:T(8,128)(2,1)S(1)}, bf16[224,192]{1,0:T(8,128)(2,1)S(1)}, u32[]{:S(2)}, u32[]{:S(2)}) %collective-permute-start.4) | collective-permute-done | bytes 86048 | tf_op jit(solution)/shard_map/ppermute | solution.py:369
  34.6 0.1 stack.1.refs_4_
  34.7 1.4 %collective-permute-start.8 = (bf16[112,5120]{1,0:T(8,128)(2,1)S(1)}, bf16[112,5120]{1,0:T(8,128)(2,1)S(1)}, u32[]{:S(2)}, u32[]{:S(2)}) collective-permute-start(bf16[112,5120]{1,0:T(8,128)(2,1)S(1)} %stack.1.refs_4_), channel_id=1, source_target_pairs={{0,2},{1,3},{4,6},{5,7},{8,10},{9,11},{12,14},{13,15},{16,18},{17,... | collective-permute-start | bytes 3440648 | tf_op jit(solution)/shard_map/ppermute | solution.py:371
  36.1 2.6 %collective-permute-start.9 = (bf16[56,5120]{1,0:T(8,128)(2,1)S(1)}, bf16[56,5120]{1,0:T(8,128)(2,1)S(1)}, u32[]{:S(2)}, u32[]{:S(2)}) collective-permute-start(bf16[56,5120]{1,0:T(8,128)(2,1)S(1)} %get-tuple-element.26), channel_id=1, source_target_pairs={{0,30},{2,0},{4,2},{6,4},{8,6},{10,8},{12,10},{14,12},{16,14},{18,... | collective-permute-start | bytes 1720328 | tf_op jit(solution)/shard_map/ppermute | solution.py:21
  38.7 0.0 copy-done.3
  38.7 1.4 %own_sums.1 = (f32[112,5120]{1,0:T(8,128)S(1)}, f32[56,5120]{1,0:T(8,128)S(1)}) custom-call(bf16[384,5120]{1,0:T(8,128)(2,1)S(1)} %copy-done.3, bf16[384,5120]{1,0:T(8,128)(2,1)S(1)} %copy-done.1, bf16[56,384]{1,0:T(8,128)(2,1)S(1)} %get-tuple-element.16.hidden_ref, bf16[112,384]{1,0:T(8,128)(2,1)S(1)} %get-tuple-element.17.after_ref.own_ref.grads_ref, ...), custom_call_target="tpu_custom_call" | custom-call | flops 660602880 | bytes 7864320 | tf_op jit(solution)/shard_map/own_sums/pallas_call | solution.py:227
  40.1 4.6 %collective-permute-done.3.back_in = bf16[112,5120]{1,0:T(8,128)(2,1)S(1)} collective-permute-done((bf16[112,5120]{1,0:T(8,128)(2,1)S(1)}, bf16[112,5120]{1,0:T(8,128)(2,1)S(1)}, u32[]{:S(2)}, u32[]{:S(2)}) %collective-permute-start.3) | collective-permute-done | bytes 1146912 | tf_op jit(solution)/shard_map/ppermute | solution.py:21
  44.8 2.9 %totals.2 = (f32[54,1,5120]{2,1,0:T(1,128)}, f32[54,1,5120]{2,1,0:T(1,128)}) custom-call(f32[112,5120]{1,0:T(8,128)S(1)} %get-tuple-element.19.own_in, bf16[112,5120]{1,0:T(8,128)(2,1)S(1)} %collective-permute-done.3.back_in, bf16[112,5120]{1,0:T(8,128)(2,1)S(1)} %get-tuple-element.18.after_ref.refs_2_), custom_call_target="tpu_custom_call" | custom-call | flops 573440 | bytes 5734400 | tf_op jit(solution)/shard_map/totals/pallas_call | solution.py:265
  47.7 1.5 %collective-permute-done.7.refs_5_ = bf16[112,5120]{1,0:T(8,128)(2,1)S(1)} collective-permute-done((bf16[112,5120]{1,0:T(8,128)(2,1)S(1)}, bf16[112,5120]{1,0:T(8,128)(2,1)S(1)}, u32[]{:S(2)}, u32[]{:S(2)}) %collective-permute-start.7) | collective-permute-done | bytes 1146912 | tf_op jit(solution)/shard_map/ppermute | solution.py:368
  49.1 0.0 collective-permute-done.8.refs_6_
  49.1 0.0 copy-start.5
  49.1 1.2 %copy-done.5 = f32[54,1,5120]{2,1,0:T(1,128)S(1)} copy-done((f32[54,1,5120]{2,1,0:T(1,128)S(1)}, f32[54,1,5120]{2,1,0:T(1,128)}, u32[]{:S(2)}) %copy-start.5) | copy-done | bytes 1105944
  50.4 2.1 %in_grad.1.after_ref = bf16[192,5120]{1,0:T(8,128)(2,1)} custom-call(f32[54,1,5120]{2,1,0:T(1,128)S(1)} %copy-done.5, bf16[224,192]{1,0:T(8,128)(2,1)S(1)} %get-tuple-element.22.refs_0_, bf16[112,5120]{1,0:T(8,128)(2,1)S(1)} %get-tuple-element.23.refs_1_, bf16[112,5120]{1,0:T(8,128)(2,1)S(1)} %get-tuple-element.18.after_ref.refs_2_, ...), custom_call_target="tpu_custom_call" | custom-call | flops 880803840 | bytes 7872512 | tf_op jit(solution)/shard_map/in_grad/pallas_call | solution.py:316
  52.5 0.0 collective-permute-done.9.back_in
  52.5 0.0 copy-start.4
  52.5 1.5 %copy-done.4 = bf16[192,5120]{1,0:T(8,128)(2,1)S(1)} copy-done((bf16[192,5120]{1,0:T(8,128)(2,1)S(1)}, bf16[192,5120]{1,0:T(8,128)(2,1)}, u32[]{:S(2)}) %copy-start.4) | copy-done | bytes 1966104
  54.1 1.8 %totals.3 = f32[54,1,5120]{2,1,0:T(1,128)} custom-call(f32[56,5120]{1,0:T(8,128)S(1)} %get-tuple-element.25.own_in, bf16[56,5120]{1,0:T(8,128)(2,1)S(1)} %collective-permute-done.9.back_in, bf16[192,5120]{1,0:T(8,128)(2,1)S(1)} %copy-done.4), custom_call_target="tpu_custom_call" | custom-call | flops 286720 | bytes 2867200 | tf_op jit(solution)/shard_map/totals/pallas_call | solution.py:265
Async XLA Ops:
  0.6 14.1 %collective-permute-start = (bf16[54,5120]{1,0:T(8,128)(2,1)}, bf16[54,5120]{1,0:T(8,128)(2,1)S(1)}, u32[]{:S(2)}, u32[]{:S(2)}) collective-permute-start(bf16[54,5120]{1,0:T(8,128)(2,1)} %bitcast.13), channel_id=1, source_target_pairs={{0,2},{2,4},{4,6},{6,8},{8,10},{10,12},{12,14},{14,16},{16,18},{18... | collective-permute-start | bytes 1658888 | tf_op jit(solution)/shard_map/ppermute | solution.py:21
  1.1 18.7 %collective-permute-start.1 = (bf16[54,5120]{1,0:T(8,128)(2,1)}, bf16[54,5120]{1,0:T(8,128)(2,1)S(1)}, u32[]{:S(2)}, u32[]{:S(2)}) collective-permute-start(bf16[54,5120]{1,0:T(8,128)(2,1)} %bitcast.15), channel_id=1, source_target_pairs={{0,2},{2,4},{4,6},{6,8},{8,10},{10,12},{12,14},{14,16},{16,18},{18... | collective-permute-start | bytes 1658888 | tf_op jit(solution)/shard_map/ppermute | solution.py:21
  3.8 22.3 %collective-permute-start.2 = (bf16[54,5120]{1,0:T(8,128)(2,1)}, bf16[54,5120]{1,0:T(8,128)(2,1)S(1)}, u32[]{:S(2)}, u32[]{:S(2)}) collective-permute-start(bf16[54,5120]{1,0:T(8,128)(2,1)} %bitcast.18), channel_id=1, source_target_pairs={{0,2},{2,4},{4,6},{6,8},{8,10},{10,12},{12,14},{14,16},{16,18},{18... | collective-permute-start | bytes 1658888 | tf_op jit(solution)/shard_map/ppermute | solution.py:21
  3.8 29.6 %collective-permute-start.5 = (bf16[54,5120]{1,0:T(8,128)(2,1)}, bf16[54,5120]{1,0:T(8,128)(2,1)S(1)}, u32[]{:S(2)}, u32[]{:S(2)}) collective-permute-start(bf16[54,5120]{1,0:T(8,128)(2,1)} %bitcast.16), channel_id=1, source_target_pairs={{0,1},{1,0},{2,3},{3,2},{4,5},{5,4},{6,7},{7,6},{8,9},{9,8},{10,11... | collective-permute-start | bytes 1658888 | tf_op jit(solution)/shard_map/ppermute | solution.py:350
  5.3 28.1 %collective-permute-start.6 = (bf16[54,5120]{1,0:T(8,128)(2,1)}, bf16[54,5120]{1,0:T(8,128)(2,1)S(1)}, u32[]{:S(2)}, u32[]{:S(2)}) collective-permute-start(bf16[54,5120]{1,0:T(8,128)(2,1)} %bitcast.19), channel_id=1, source_target_pairs={{0,1},{1,0},{2,3},{3,2},{4,5},{5,4},{6,7},{7,6},{8,9},{9,8},{10,11... | collective-permute-start | bytes 1658888 | tf_op jit(solution)/shard_map/ppermute | solution.py:350
  5.9 2.1 %copy-start = (bf16[384,5120]{1,0:T(8,128)(2,1)S(1)}, bf16[384,5120]{1,0:T(8,128)(2,1)}, u32[]{:S(2)}) copy-start(bf16[384,5120]{1,0:T(8,128)(2,1)} %g_ref.7) | copy-start | bytes 11796484
  8.0 2.1 %copy-start.2 = (bf16[384,5120]{1,0:T(8,128)(2,1)S(1)}, bf16[384,5120]{1,0:T(8,128)(2,1)}, u32[]{:S(2)}) copy-start(bf16[384,5120]{1,0:T(8,128)(2,1)} %x_ref.5) | copy-start | bytes 11796484
  10.1 4.6 %copy-start.1 = (bf16[384,5120]{1,0:T(8,128)(2,1)S(1)}, bf16[384,5120]{1,0:T(8,128)(2,1)}, u32[]{:S(2)}) copy-start(bf16[384,5120]{1,0:T(8,128)(2,1)} %g_ref.7) | copy-start | bytes 11796484
  26.0 12.7 %copy-start.3 = (bf16[384,5120]{1,0:T(8,128)(2,1)S(1)}, bf16[384,5120]{1,0:T(8,128)(2,1)}, u32[]{:S(2)}) copy-start(bf16[384,5120]{1,0:T(8,128)(2,1)} %x_ref.5) | copy-start | bytes 11796484
  29.4 5.3 %collective-permute-start.4 = (bf16[224,192]{1,0:T(8,128)(2,1)S(1)}, bf16[224,192]{1,0:T(8,128)(2,1)S(1)}, u32[]{:S(2)}, u32[]{:S(2)}) collective-permute-start(bf16[224,192]{1,0:T(8,128)(2,1)S(1)} %get-tuple-element.24), channel_id=1, source_target_pairs={{0,1},{1,0},{2,3},{3,2},{4,5},{5,4},{6,7},{7,6},{8,9},{9,8},{10,11... | collective-permute-start | bytes 258056 | tf_op jit(solution)/shard_map/ppermute | solution.py:369
  31.4 13.4 %collective-permute-start.3 = (bf16[112,5120]{1,0:T(8,128)(2,1)S(1)}, bf16[112,5120]{1,0:T(8,128)(2,1)S(1)}, u32[]{:S(2)}, u32[]{:S(2)}) collective-permute-start(bf16[112,5120]{1,0:T(8,128)(2,1)S(1)} %get-tuple-element.20), channel_id=1, source_target_pairs={{0,30},{2,0},{4,2},{6,4},{8,6},{10,8},{12,10},{14,12},{16,14},{18,... | collective-permute-start | bytes 3440648 | tf_op jit(solution)/shard_map/ppermute | solution.py:21
  31.4 17.7 %collective-permute-start.7 = (bf16[112,5120]{1,0:T(8,128)(2,1)S(1)}, bf16[112,5120]{1,0:T(8,128)(2,1)S(1)}, u32[]{:S(2)}, u32[]{:S(2)}) collective-permute-start(bf16[112,5120]{1,0:T(8,128)(2,1)S(1)} %get-tuple-element.18.after_ref.refs_2_), channel_id=1, source_target_pairs={{0,1},{1,0},{4,5},{5,4},{8,9},{9,8},{12,13},{13,12},{16,17},{17,16... | collective-permute-start | bytes 3440648 | tf_op jit(solution)/shard_map/ppermute | solution.py:368
  34.7 14.4 %collective-permute-start.8 = (bf16[112,5120]{1,0:T(8,128)(2,1)S(1)}, bf16[112,5120]{1,0:T(8,128)(2,1)S(1)}, u32[]{:S(2)}, u32[]{:S(2)}) collective-permute-start(bf16[112,5120]{1,0:T(8,128)(2,1)S(1)} %stack.1.refs_4_), channel_id=1, source_target_pairs={{0,2},{1,3},{4,6},{5,7},{8,10},{9,11},{12,14},{13,15},{16,18},{17,... | collective-permute-start | bytes 3440648 | tf_op jit(solution)/shard_map/ppermute | solution.py:371
  36.1 16.4 %collective-permute-start.9 = (bf16[56,5120]{1,0:T(8,128)(2,1)S(1)}, bf16[56,5120]{1,0:T(8,128)(2,1)S(1)}, u32[]{:S(2)}, u32[]{:S(2)}) collective-permute-start(bf16[56,5120]{1,0:T(8,128)(2,1)S(1)} %get-tuple-element.26), channel_id=1, source_target_pairs={{0,30},{2,0},{4,2},{6,4},{8,6},{10,8},{12,10},{14,12},{16,14},{18,... | collective-permute-start | bytes 1720328 | tf_op jit(solution)/shard_map/ppermute | solution.py:21
  49.1 1.2 %copy-start.5 = (f32[54,1,5120]{2,1,0:T(1,128)S(1)}, f32[54,1,5120]{2,1,0:T(1,128)}, u32[]{:S(2)}) copy-start(f32[54,1,5120]{2,1,0:T(1,128)} %get-tuple-element.21.after_ref) | copy-start | bytes 3317764
  52.5 1.5 %copy-start.4 = (bf16[192,5120]{1,0:T(8,128)(2,1)S(1)}, bf16[192,5120]{1,0:T(8,128)(2,1)}, u32[]{:S(2)}) copy-start(bf16[192,5120]{1,0:T(8,128)(2,1)} %in_grad.1.after_ref) | copy-start | bytes 5898244
where the time goes:
time: 56.1 us; the launch traced here: 55.8 us
  Pallas kernels  17.5 us (31%)
  waiting for transfers between devices  17.3 us (31%)
  starting transfers between devices  13.2 us (24%)
  local copies, waits for them, and re-layouts  7.02 us (13%)
  between operations  0.76 us (1%)
    ppermute x5, waiting for transfers between devices, from_behind(): lax.ppermute(value, axis, [(i, (i + by) % devices) for i in range(devices)])  14.6 us
    unnamed x12, local copies, waits for them, and re-layouts  7.02 us
    ppermute x5, starting transfers between devices, from_behind(): lax.ppermute(value, axis, [(i, (i + by) % devices) for i in range(devices)])  5.83 us
    pallas_call x2, Pallas kernels, totals(): pl.pallas_call(total_kernel, in_specs=[ANY] * 3, out_specs=[HBM] * count,...  4.63 us
    pallas_call x1, Pallas kernels, own_meeting(): pl.pallas_call(own_kernel, in_specs=[VMEM] * 2 + [HBM] * 3, out_specs=[VM...  4.59 us
    pallas_call x1, Pallas kernels, second_meeting(): pl.pallas_call(functools.partial(second_kernel, n_stacks, halves), in_spe...  3.35 us
    pallas_call x1, Pallas kernels, in_grad_of(): pl.pallas_call(functools.partial(in_grad_kernel, [len(l) for l, _ in part...  2.13 us
    ppermute x2, starting transfers between devices, local(): lax.ppermute(w, 'tensor', swap)  2.03 us
  transfers between devices with their start and end apart: 10, of which 5 were waited for; matrix products, arithmetic and copies ran while one was open for 0% of the time, Pallas kernels for 28%

commit v1 on v0

--- a/solution.py
+++ b/solution.py
@@ -264,7 +264,7 @@
     rows, width = own.shape
     return pl.pallas_call(
         total_kernel,
-        in_specs=[ANY] * 3,
+        in_specs=[ANY, ANY, HBM],
         out_specs=[HBM] * count,
         out_shape=[jax.ShapeDtypeStruct((hidden, 1, width), F32)] * count,
         scratch_shapes=[
@@ -275,7 +275,7 @@
         ],
         name="totals",
         **params(rows * width, 10 * rows * width),
-    )(own, back, after)
+    )(own, back, pltpu.with_memory_space_constraint(after, pltpu.HBM))
 
 
 def in_grad_kernel(left_counts, right_counts, after_ref, *refs):
@@ -319,7 +319,7 @@
             [len(l) for l, _ in partials],
             [[len(t) for t in r] for _, r in partials],
         ),
-        in_specs=[ANY] + [VMEM] * len(operands),
+        in_specs=[HBM] + [VMEM] * len(operands),
         out_specs=HBM,
         out_shape=jax.ShapeDtypeStruct((rows, width), BF16),
         scratch_shapes=[
@@ -331,7 +331,7 @@
             2 * sum(t.shape[0] for l, _ in partials for t in l) * rows * width,
             2 * sum(t.size for t in operands) + 2 * rows * width,
         ),
-    )(after, *in_vmem(*operands))
+    )(pltpu.with_memory_space_constraint(after, pltpu.HBM), *in_vmem(*operands))
 
 
 def local(activations, out_grad, gate_weight, up_weight, down_weight):
@@ -362,7 +362,7 @@
     )
     back_early, back_late = [from_behind(t, "blk", -1) for t in (early, late)]
     sums_early, sums_late = own_sums(activations, out_grad, own_hidden, own_grads, prev_gu)
-    total_down, total_gate = totals(sums_early, back_early, 2, hidden, prev_gu)
+    total_down, total_gate = totals(sums_early, back_early, 2, hidden, activations)
     if pairs:
         mine, sent = grads
         prev_other_even = lax.ppermute(prev_gu, axes, across)
@@ -376,7 +376,7 @@
         )
         after = in_grad
     else:
-        after = in_grad_of(prev_gu, (grads, [[w_gu], [prev_gu]]))
+        after = in_grad_of(activations, (grads, [[w_gu], [prev_gu]]))
         in_grad = lax.psum_scatter(after, "tensor", scatter_dimension=0, tiled=True)
     [total_up] = totals(sums_late, back_late, 1, hidden, after)
     return (

time: 56.1 us -> 53.3 us (0.950)
  local copies, waits for them, and re-layouts: 7.02 us -> 4.24 us
    unnamed x12 -> x8, local copies, waits for them, and re-layouts: 7.02 us -> 4.24 us
  transfers between devices with their start and end apart: 10 -> 10, of which waited for: 5 -> 5; matrix products, arithmetic and copies ran while one was open for 0% -> 0% of each run, Pallas kernels for 28% -> 30%
where the time goes in v1:
time: 53.3 us; the launch traced here: 53 us
  Pallas kernels  17.5 us (33%)
  waiting for transfers between devices  17.3 us (32%)
  starting transfers between devices  13.2 us (25%)
  local copies, waits for them, and re-layouts  4.24 us (8%)
  between operations  0.76 us (1%)
    ppermute x5, waiting for transfers between devices, from_behind(): lax.ppermute(value, axis, [(i, (i + by) % devices) for i in range(devices)])  14.6 us
    ppermute x5, starting transfers between devices, from_behind(): lax.ppermute(value, axis, [(i, (i + by) % devices) for i in range(devices)])  5.85 us
    pallas_call x2, Pallas kernels, totals(): pl.pallas_call(total_kernel, in_specs=[ANY, ANY, HBM], out_specs=[HBM] *...  4.64 us
    pallas_call x1, Pallas kernels, own_meeting(): pl.pallas_call(own_kernel, in_specs=[VMEM] * 2 + [HBM] * 3, out_specs=[VM...  4.59 us
    unnamed x8, local copies, waits for them, and re-layouts  4.24 us
    pallas_call x1, Pallas kernels, second_meeting(): pl.pallas_call(functools.partial(second_kernel, n_stacks, halves), in_spe...  3.36 us
    pallas_call x1, Pallas kernels, in_grad_of(): pl.pallas_call(functools.partial(in_grad_kernel, [len(l) for l, _ in part...  2.11 us
    ppermute x2, starting transfers between devices, local(): lax.ppermute(w, 'tensor', swap)  2.03 us
  transfers between devices with their start and end apart: 10, of which 5 were waited for; matrix products, arithmetic and copies ran while one was open for 0% of the time, Pallas kernels for 30%

profile of v1, /device:TPU:0, one launch (start us, length us, event | category | flops | bytes accessed | tf_op | source)
XLA Modules:
  0.0 53.0 jit_solution(1296130066902022621)
XLA Ops:
  0.6 0.5 collective-permute-start
  1.1 2.6 %collective-permute-start.1 = (bf16[54,5120]{1,0:T(8,128)(2,1)}, bf16[54,5120]{1,0:T(8,128)(2,1)S(1)}, u32[]{:S(2)}, u32[]{:S(2)}) collective-permute-start(bf16[54,5120]{1,0:T(8,128)(2,1)} %bitcast.15), channel_id=1, source_target_pairs={{0,2},{2,4},{4,6},{6,8},{8,10},{10,12},{12,14},{14,16},{16,18},{18... | collective-permute-start | bytes 1658888 | tf_op jit(solution)/shard_map/ppermute | solution.py:21
  3.8 0.1 collective-permute-start.2
  3.8 1.5 %collective-permute-start.5 = (bf16[54,5120]{1,0:T(8,128)(2,1)}, bf16[54,5120]{1,0:T(8,128)(2,1)S(1)}, u32[]{:S(2)}, u32[]{:S(2)}) collective-permute-start(bf16[54,5120]{1,0:T(8,128)(2,1)} %bitcast.16), channel_id=1, source_target_pairs={{0,1},{1,0},{2,3},{3,2},{4,5},{5,4},{6,7},{7,6},{8,9},{9,8},{10,11... | collective-permute-start | bytes 1658888 | tf_op jit(solution)/shard_map/ppermute | solution.py:350
  5.3 0.5 %collective-permute-start.6 = (bf16[54,5120]{1,0:T(8,128)(2,1)}, bf16[54,5120]{1,0:T(8,128)(2,1)S(1)}, u32[]{:S(2)}, u32[]{:S(2)}) collective-permute-start(bf16[54,5120]{1,0:T(8,128)(2,1)} %bitcast.19), channel_id=1, source_target_pairs={{0,1},{1,0},{2,3},{3,2},{4,5},{5,4},{6,7},{7,6},{8,9},{9,8},{10,11... | collective-permute-start | bytes 1658888 | tf_op jit(solution)/shard_map/ppermute | solution.py:350
  5.9 0.0 copy-start
  5.9 2.1 %copy-done = bf16[384,5120]{1,0:T(8,128)(2,1)S(1)} copy-done((bf16[384,5120]{1,0:T(8,128)(2,1)S(1)}, bf16[384,5120]{1,0:T(8,128)(2,1)}, u32[]{:S(2)}) %copy-start) | copy-done | bytes 3932184
  8.0 0.0 copy-start.2
  8.0 2.1 %copy-done.2 = bf16[384,5120]{1,0:T(8,128)(2,1)S(1)} copy-done((bf16[384,5120]{1,0:T(8,128)(2,1)S(1)}, bf16[384,5120]{1,0:T(8,128)(2,1)}, u32[]{:S(2)}) %copy-start.2) | copy-done | bytes 3932184
  10.1 0.0 copy-start.3
  10.1 4.6 %own_meeting.1 = (bf16[112,5120]{1,0:T(8,128)(2,1)S(1)}, bf16[112,384]{1,0:T(8,128)(2,1)S(1)}, bf16[56,384]{1,0:T(8,128)(2,1)S(1)}) custom-call(bf16[384,5120]{1,0:T(8,128)(2,1)S(1)} %copy-done, bf16[384,5120]{1,0:T(8,128)(2,1)S(1)} %copy-done.2, bf16[54,5120]{1,0:T(8,128)(2,1)} %bitcast.17, bf16[54,5120]{1,0:T(8,128)(2,1)} %bitcast.20, ...), custom_call_target="tpu_custom_call" | custom-call | flops 660602880 | bytes 7864320 | tf_op jit(solution)/shard_map/own_meeting/pallas_call | solution.py:125
  14.7 0.0 collective-permute-done.down_ref
  14.7 0.0 copy-done.3
  14.7 0.0 copy-start.1
  14.7 1.3 %grad_hidden.1.prev_ref = f32[54,384]{1,0:T(8,128)S(1)} custom-call(bf16[384,5120]{1,0:T(8,128)(2,1)S(1)} %copy-done.3, bf16[54,5120]{1,0:T(8,128)(2,1)S(1)} %collective-permute-done.down_ref, bf16[112,384]{1,0:T(8,128)(2,1)S(1)} %get-tuple-element.17.after_ref.own_ref.grads_ref), custom_call_target="tpu_custom_call" | custom-call | flops 212336640 | bytes 3932160 | tf_op jit(solution)/shard_map/grad_hidden/pallas_call | solution.py:147
  16.0 3.8 %collective-permute-done.1.refs_0_ = bf16[54,5120]{1,0:T(8,128)(2,1)S(1)} collective-permute-done((bf16[54,5120]{1,0:T(8,128)(2,1)}, bf16[54,5120]{1,0:T(8,128)(2,1)S(1)}, u32[]{:S(2)}, u32[]{:S(2)}) %collective-permute-start.1) | collective-permute-done | bytes 552992 | tf_op jit(solution)/shard_map/ppermute | solution.py:21
  19.9 6.1 %collective-permute-done.2.refs_1_ = bf16[54,5120]{1,0:T(8,128)(2,1)S(1)} collective-permute-done((bf16[54,5120]{1,0:T(8,128)(2,1)}, bf16[54,5120]{1,0:T(8,128)(2,1)S(1)}, u32[]{:S(2)}, u32[]{:S(2)}) %collective-permute-start.2) | collective-permute-done | bytes 552992 | tf_op jit(solution)/shard_map/ppermute | solution.py:21
  26.0 0.0 copy-done.1
  26.0 3.4 %second_meeting.1 = (bf16[112,5120]{1,0:T(8,128)(2,1)S(1)}, bf16[56,5120]{1,0:T(8,128)(2,1)S(1)}, bf16[112,5120]{1,0:T(8,128)(2,1)S(1)}, bf16[224,192]{1,0:T(8,128)(2,1)S(1)}, bf16[224,192]{1,0:T(8,128)(2,1)S(1)}) custom-call(bf16[384,5120]{1,0:T(8,128)(2,1)S(1)} %copy-done.1, bf16[384,5120]{1,0:T(8,128)(2,1)S(1)} %copy-done.3, ...), custom_call_target="tpu_custom_call" | custom-call | flops 1321205760 | bytes 7864320 | tf_op jit(solution)/shard_map/second_meeting/pallas_call | solution.py:190
  29.4 2.0 %collective-permute-start.4 = (bf16[224,192]{1,0:T(8,128)(2,1)S(1)}, bf16[224,192]{1,0:T(8,128)(2,1)S(1)}, u32[]{:S(2)}, u32[]{:S(2)}) collective-permute-start(bf16[224,192]{1,0:T(8,128)(2,1)S(1)} %get-tuple-element.24), channel_id=1, source_target_pairs={{0,1},{1,0},{2,3},{3,2},{4,5},{5,4},{6,7},{7,6},{8,9},{9,8},{10,11... | collective-permute-start | bytes 258056 | tf_op jit(solution)/shard_map/ppermute | solution.py:369
  31.4 0.0 collective-permute-start.3
  31.4 2.0 %collective-permute-start.7 = (bf16[112,5120]{1,0:T(8,128)(2,1)S(1)}, bf16[112,5120]{1,0:T(8,128)(2,1)S(1)}, u32[]{:S(2)}, u32[]{:S(2)}) collective-permute-start(bf16[112,5120]{1,0:T(8,128)(2,1)S(1)} %get-tuple-element.18.after_ref.refs_2_), channel_id=1, source_target_pairs={{0,1},{1,0},{4,5},{5,4},{8,9},{9,8},{12,13},{13,12},{16,17},{17,16... | collective-permute-start | bytes 3440648 | tf_op jit(solution)/shard_map/ppermute | solution.py:368
  33.4 0.0 collective-permute-done.5.gate_ref
  33.4 0.0 collective-permute-done.6.up_ref
  33.4 1.2 %collective-permute-done.4.after_ref.refs_3_ = bf16[224,192]{1,0:T(8,128)(2,1)S(1)} collective-permute-done((bf16[224,192]{1,0:T(8,128)(2,1)S(1)}, bf16[224,192]{1,0:T(8,128)(2,1)S(1)}, u32[]{:S(2)}, u32[]{:S(2)}) %collective-permute-start.4) | collective-permute-done | bytes 86048 | tf_op jit(solution)/shard_map/ppermute | solution.py:369
  34.6 0.1 stack.1.refs_4_
  34.7 1.4 %collective-permute-start.8 = (bf16[112,5120]{1,0:T(8,128)(2,1)S(1)}, bf16[112,5120]{1,0:T(8,128)(2,1)S(1)}, u32[]{:S(2)}, u32[]{:S(2)}) collective-permute-start(bf16[112,5120]{1,0:T(8,128)(2,1)S(1)} %stack.1.refs_4_), channel_id=1, source_target_pairs={{0,2},{1,3},{4,6},{5,7},{8,10},{9,11},{12,14},{13,15},{16,18},{17,... | collective-permute-start | bytes 3440648 | tf_op jit(solution)/shard_map/ppermute | solution.py:371
  36.1 2.6 %collective-permute-start.9 = (bf16[56,5120]{1,0:T(8,128)(2,1)S(1)}, bf16[56,5120]{1,0:T(8,128)(2,1)S(1)}, u32[]{:S(2)}, u32[]{:S(2)}) collective-permute-start(bf16[56,5120]{1,0:T(8,128)(2,1)S(1)} %get-tuple-element.26), channel_id=1, source_target_pairs={{0,30},{2,0},{4,2},{6,4},{8,6},{10,8},{12,10},{14,12},{16,14},{18,... | collective-permute-start | bytes 1720328 | tf_op jit(solution)/shard_map/ppermute | solution.py:21
  38.7 1.4 %own_sums.1 = (f32[112,5120]{1,0:T(8,128)S(1)}, f32[56,5120]{1,0:T(8,128)S(1)}) custom-call(bf16[384,5120]{1,0:T(8,128)(2,1)S(1)} %copy-done.1, bf16[384,5120]{1,0:T(8,128)(2,1)S(1)} %copy-done.3, bf16[56,384]{1,0:T(8,128)(2,1)S(1)} %get-tuple-element.16.hidden_ref, bf16[112,384]{1,0:T(8,128)(2,1)S(1)} %get-tuple-element.17.after_ref.own_ref.grads_ref, ...), custom_call_target="tpu_custom_call" | custom-call | flops 660602880 | bytes 7864320 | tf_op jit(solution)/shard_map/own_sums/pallas_call | solution.py:227
  40.2 4.6 %collective-permute-done.3.back_in = bf16[112,5120]{1,0:T(8,128)(2,1)S(1)} collective-permute-done((bf16[112,5120]{1,0:T(8,128)(2,1)S(1)}, bf16[112,5120]{1,0:T(8,128)(2,1)S(1)}, u32[]{:S(2)}, u32[]{:S(2)}) %collective-permute-start.3) | collective-permute-done | bytes 1146912 | tf_op jit(solution)/shard_map/ppermute | solution.py:21
  44.8 2.9 %totals.2 = (f32[54,1,5120]{2,1,0:T(1,128)}, f32[54,1,5120]{2,1,0:T(1,128)}) custom-call(f32[112,5120]{1,0:T(8,128)S(1)} %get-tuple-element.19.own_in, bf16[112,5120]{1,0:T(8,128)(2,1)S(1)} %collective-permute-done.3.back_in, bf16[384,5120]{1,0:T(8,128)(2,1)} %after_ref.1), custom_call_target="tpu_custom_call" | custom-call | flops 573440 | bytes 5734400 | tf_op jit(solution)/shard_map/totals/pallas_call | solution.py:265
  47.7 1.5 %collective-permute-done.7.refs_5_ = bf16[112,5120]{1,0:T(8,128)(2,1)S(1)} collective-permute-done((bf16[112,5120]{1,0:T(8,128)(2,1)S(1)}, bf16[112,5120]{1,0:T(8,128)(2,1)S(1)}, u32[]{:S(2)}, u32[]{:S(2)}) %collective-permute-start.7) | collective-permute-done | bytes 1146912 | tf_op jit(solution)/shard_map/ppermute | solution.py:368
  49.1 0.0 collective-permute-done.8.refs_6_
  49.1 2.1 %in_grad.1.after_ref = bf16[192,5120]{1,0:T(8,128)(2,1)} custom-call(f32[54,1,5120]{2,1,0:T(1,128)} %get-tuple-element.21.after_ref, bf16[224,192]{1,0:T(8,128)(2,1)S(1)} %get-tuple-element.22.refs_0_, bf16[112,5120]{1,0:T(8,128)(2,1)S(1)} %get-tuple-element.23.refs_1_, bf16[112,5120]{1,0:T(8,128)(2,1)S(1)} %get-tuple-element.18.after_ref.refs_2_, ...), custom_call_target="tpu_custom_call" | custom-call | flops 880803840 | bytes 7872512 | tf_op jit(solution)/shard_map/in_grad/pallas_call | solution.py:316
  51.3 0.0 collective-permute-done.9.back_in
  51.3 1.8 %totals.3 = f32[54,1,5120]{2,1,0:T(1,128)} custom-call(f32[56,5120]{1,0:T(8,128)S(1)} %get-tuple-element.25.own_in, bf16[56,5120]{1,0:T(8,128)(2,1)S(1)} %collective-permute-done.9.back_in, bf16[192,5120]{1,0:T(8,128)(2,1)} %in_grad.1.after_ref), custom_call_target="tpu_custom_call" | custom-call | flops 286720 | bytes 2867200 | tf_op jit(solution)/shard_map/totals/pallas_call | solution.py:265
Async XLA Ops:
  0.6 14.1 %collective-permute-start = (bf16[54,5120]{1,0:T(8,128)(2,1)}, bf16[54,5120]{1,0:T(8,128)(2,1)S(1)}, u32[]{:S(2)}, u32[]{:S(2)}) collective-permute-start(bf16[54,5120]{1,0:T(8,128)(2,1)} %bitcast.13), channel_id=1, source_target_pairs={{0,2},{2,4},{4,6},{6,8},{8,10},{10,12},{12,14},{14,16},{16,18},{18... | collective-permute-start | bytes 1658888 | tf_op jit(solution)/shard_map/ppermute | solution.py:21
  1.1 18.7 %collective-permute-start.1 = (bf16[54,5120]{1,0:T(8,128)(2,1)}, bf16[54,5120]{1,0:T(8,128)(2,1)S(1)}, u32[]{:S(2)}, u32[]{:S(2)}) collective-permute-start(bf16[54,5120]{1,0:T(8,128)(2,1)} %bitcast.15), channel_id=1, source_target_pairs={{0,2},{2,4},{4,6},{6,8},{8,10},{10,12},{12,14},{14,16},{16,18},{18... | collective-permute-start | bytes 1658888 | tf_op jit(solution)/shard_map/ppermute | solution.py:21
  3.8 22.3 %collective-permute-start.2 = (bf16[54,5120]{1,0:T(8,128)(2,1)}, bf16[54,5120]{1,0:T(8,128)(2,1)S(1)}, u32[]{:S(2)}, u32[]{:S(2)}) collective-permute-start(bf16[54,5120]{1,0:T(8,128)(2,1)} %bitcast.18), channel_id=1, source_target_pairs={{0,2},{2,4},{4,6},{6,8},{8,10},{10,12},{12,14},{14,16},{16,18},{18... | collective-permute-start | bytes 1658888 | tf_op jit(solution)/shard_map/ppermute | solution.py:21
  3.8 29.6 %collective-permute-start.5 = (bf16[54,5120]{1,0:T(8,128)(2,1)}, bf16[54,5120]{1,0:T(8,128)(2,1)S(1)}, u32[]{:S(2)}, u32[]{:S(2)}) collective-permute-start(bf16[54,5120]{1,0:T(8,128)(2,1)} %bitcast.16), channel_id=1, source_target_pairs={{0,1},{1,0},{2,3},{3,2},{4,5},{5,4},{6,7},{7,6},{8,9},{9,8},{10,11... | collective-permute-start | bytes 1658888 | tf_op jit(solution)/shard_map/ppermute | solution.py:350
  5.3 28.1 %collective-permute-start.6 = (bf16[54,5120]{1,0:T(8,128)(2,1)}, bf16[54,5120]{1,0:T(8,128)(2,1)S(1)}, u32[]{:S(2)}, u32[]{:S(2)}) collective-permute-start(bf16[54,5120]{1,0:T(8,128)(2,1)} %bitcast.19), channel_id=1, source_target_pairs={{0,1},{1,0},{2,3},{3,2},{4,5},{5,4},{6,7},{7,6},{8,9},{9,8},{10,11... | collective-permute-start | bytes 1658888 | tf_op jit(solution)/shard_map/ppermute | solution.py:350
  5.9 2.1 %copy-start = (bf16[384,5120]{1,0:T(8,128)(2,1)S(1)}, bf16[384,5120]{1,0:T(8,128)(2,1)}, u32[]{:S(2)}) copy-start(bf16[384,5120]{1,0:T(8,128)(2,1)} %after_ref.1) | copy-start | bytes 11796484
  8.0 2.1 %copy-start.2 = (bf16[384,5120]{1,0:T(8,128)(2,1)S(1)}, bf16[384,5120]{1,0:T(8,128)(2,1)}, u32[]{:S(2)}) copy-start(bf16[384,5120]{1,0:T(8,128)(2,1)} %g_ref.7) | copy-start | bytes 11796484
  10.1 4.6 %copy-start.3 = (bf16[384,5120]{1,0:T(8,128)(2,1)S(1)}, bf16[384,5120]{1,0:T(8,128)(2,1)}, u32[]{:S(2)}) copy-start(bf16[384,5120]{1,0:T(8,128)(2,1)} %g_ref.7) | copy-start | bytes 11796484
  14.7 11.3 %copy-start.1 = (bf16[384,5120]{1,0:T(8,128)(2,1)S(1)}, bf16[384,5120]{1,0:T(8,128)(2,1)}, u32[]{:S(2)}) copy-start(bf16[384,5120]{1,0:T(8,128)(2,1)} %after_ref.1) | copy-start | bytes 11796484
  29.4 5.3 %collective-permute-start.4 = (bf16[224,192]{1,0:T(8,128)(2,1)S(1)}, bf16[224,192]{1,0:T(8,128)(2,1)S(1)}, u32[]{:S(2)}, u32[]{:S(2)}) collective-permute-start(bf16[224,192]{1,0:T(8,128)(2,1)S(1)} %get-tuple-element.24), channel_id=1, source_target_pairs={{0,1},{1,0},{2,3},{3,2},{4,5},{5,4},{6,7},{7,6},{8,9},{9,8},{10,11... | collective-permute-start | bytes 258056 | tf_op jit(solution)/shard_map/ppermute | solution.py:369
  31.4 13.4 %collective-permute-start.3 = (bf16[112,5120]{1,0:T(8,128)(2,1)S(1)}, bf16[112,5120]{1,0:T(8,128)(2,1)S(1)}, u32[]{:S(2)}, u32[]{:S(2)}) collective-permute-start(bf16[112,5120]{1,0:T(8,128)(2,1)S(1)} %get-tuple-element.20), channel_id=1, source_target_pairs={{0,30},{2,0},{4,2},{6,4},{8,6},{10,8},{12,10},{14,12},{16,14},{18,... | collective-permute-start | bytes 3440648 | tf_op jit(solution)/shard_map/ppermute | solution.py:21
  31.4 17.7 %collective-permute-start.7 = (bf16[112,5120]{1,0:T(8,128)(2,1)S(1)}, bf16[112,5120]{1,0:T(8,128)(2,1)S(1)}, u32[]{:S(2)}, u32[]{:S(2)}) collective-permute-start(bf16[112,5120]{1,0:T(8,128)(2,1)S(1)} %get-tuple-element.18.after_ref.refs_2_), channel_id=1, source_target_pairs={{0,1},{1,0},{4,5},{5,4},{8,9},{9,8},{12,13},{13,12},{16,17},{17,16... | collective-permute-start | bytes 3440648 | tf_op jit(solution)/shard_map/ppermute | solution.py:368
  34.7 14.4 %collective-permute-start.8 = (bf16[112,5120]{1,0:T(8,128)(2,1)S(1)}, bf16[112,5120]{1,0:T(8,128)(2,1)S(1)}, u32[]{:S(2)}, u32[]{:S(2)}) collective-permute-start(bf16[112,5120]{1,0:T(8,128)(2,1)S(1)} %stack.1.refs_4_), channel_id=1, source_target_pairs={{0,2},{1,3},{4,6},{5,7},{8,10},{9,11},{12,14},{13,15},{16,18},{17,... | collective-permute-start | bytes 3440648 | tf_op jit(solution)/shard_map/ppermute | solution.py:371
  36.1 15.2 %collective-permute-start.9 = (bf16[56,5120]{1,0:T(8,128)(2,1)S(1)}, bf16[56,5120]{1,0:T(8,128)(2,1)S(1)}, u32[]{:S(2)}, u32[]{:S(2)}) collective-permute-start(bf16[56,5120]{1,0:T(8,128)(2,1)S(1)} %get-tuple-element.26), channel_id=1, source_target_pairs={{0,30},{2,0},{4,2},{6,4},{8,6},{10,8},{12,10},{14,12},{16,14},{18,... | collective-permute-start | bytes 1720328 | tf_op jit(solution)/shard_map/ppermute | solution.py:21

commit v2 on v1

--- a/solution.py
+++ b/solution.py
@@ -234,48 +234,37 @@
     )(*in_vmem(x, g, hidden, grads), after)
 
 
-def total_kernel(own_in, back_in, after_ref, *refs):
-    del after_ref
-    out_refs, (own_ref, back_ref, in_sem, out_sem) = refs[:-4], refs[-4:]
+def total_kernel(own_ref, back_ref, after_ref, *refs):
+    del after_ref
+    out_refs, (total_ref, sem) = refs[:-2], refs[-2:]
     step, hidden = own_ref.shape[0] // len(out_refs), out_refs[0].shape[0]
-    rows = [pl.ds(k * step, step) for k in range(len(out_refs))]
-    loads = [pltpu.make_async_copy(back_in, back_ref, in_sem.at[0])] + [
-        pltpu.make_async_copy(own_in.at[at, :], own_ref.at[at, :], in_sem.at[1 + k])
-        for k, at in enumerate(rows)
-    ]
-    for copy in loads:
-        copy.start()
-    loads[0].wait()
     stores = []
-    for k, at in enumerate(rows):
-        loads[1 + k].wait()
+    for k, out_ref in enumerate(out_refs):
         for first in range(0, step, 8):
             part = pl.ds(k * step + first, 8)
-            own_ref[part, :] = own_ref[part, :] + back_ref[part, :].astype(F32)
+            total_ref[part, :] = own_ref[part, :] + back_ref[part, :].astype(F32)
             for r in range(first, min(first + 8, hidden)):
-                row = own_ref.at[pl.ds(k * step + r, 1), :]
-                stores.append(pltpu.make_async_copy(row, out_refs[k].at[r], out_sem.at[k, r]))
+                row = total_ref.at[pl.ds(k * step + r, 1), :]
+                stores.append(pltpu.make_async_copy(row, out_ref.at[r], sem.at[k, r]))
                 stores[-1].start()
     for copy in stores:
         copy.wait()
 
 
-def totals(own, back, count, hidden, after):
+def totals(own, back, count, hidden, after, place=HBM):
     rows, width = own.shape
     return pl.pallas_call(
         total_kernel,
-        in_specs=[ANY, ANY, HBM],
+        in_specs=[VMEM, VMEM, place],
         out_specs=[HBM] * count,
         out_shape=[jax.ShapeDtypeStruct((hidden, 1, width), F32)] * count,
         scratch_shapes=[
             pltpu.VMEM((rows, width), F32),
-            pltpu.VMEM((rows, width), BF16),
-            pltpu.SemaphoreType.DMA((1 + count,)),
             pltpu.SemaphoreType.DMA((count, hidden)),
         ],
         name="totals",
         **params(rows * width, 10 * rows * width),
-    )(own, back, pltpu.with_memory_space_constraint(after, pltpu.HBM))
+    )(*in_vmem(own, back), pltpu.with_memory_space_constraint(after, pltpu.HBM) if place is HBM else after)
 
 
 def in_grad_kernel(left_counts, right_counts, after_ref, *refs):
@@ -334,6 +323,68 @@
     )(pltpu.with_memory_space_constraint(after, pltpu.HBM), *in_vmem(*operands))
 
 
+def dot_left(left, right):
+    return lax.dot_general(left, right, (((0,), (0,)), ((), ())), preferred_element_type=F32)
+
+
+def ready_part_kernel(mine_ref, own_ref, prev_ref, theirs_ref, other_ref, after_ref, mine_out, theirs_out, done_ref):
+    del after_ref
+    step2 = other_ref.shape[0]
+    done_ref[...] = jnp.zeros_like(done_ref)
+    for at in columns(own_ref.shape[1]):
+        both = jnp.concatenate([own_ref[:, at], prev_ref[:, at]], axis=0)
+        mine_out[:, at] = dot_left(mine_ref[...], both).astype(BF16)
+        theirs_out[:, at] = dot_left(theirs_ref[:step2, :], other_ref[:, at])
+
+
+def ready_part(mine, own, prev, theirs, other, after):
+    rows, width = mine.shape[1], own.shape[1]
+    return pl.pallas_call(
+        ready_part_kernel,
+        in_specs=[VMEM] * 5 + [ANY],
+        out_specs=[VMEM] * 3,
+        out_shape=[
+            pltpu.VMEM((rows, width), BF16),
+            pltpu.VMEM((rows, width), F32),
+            pltpu.VMEM((8, 128), F32),
+        ],
+        name="ready_part",
+        **params(6 * other.shape[0] * rows * width, 6 * rows * width),
+    )(*in_vmem(mine, own, prev, theirs, other), after)
+
+
+def last_part_kernel(mine_ref, part_ref, theirs_ref, even_ref, odd_ref, after_ref, out_ref, scratch, sem):
+    del after_ref
+    stores = []
+    for n, at in enumerate(columns(out_ref.shape[1])):
+        term = dot_left(theirs_ref[even_ref.shape[0] :, :], even_ref[:, at] + odd_ref[:, at])
+        theirs = (part_ref[:, at] + term).astype(BF16)
+        scratch[:, at] = (mine_ref[:, at].astype(F32) + theirs.astype(F32)).astype(BF16)
+        stores.append(pltpu.make_async_copy(scratch.at[:, at], out_ref.at[:, at], sem.at[n]))
+        stores[-1].start()
+    for copy in stores:
+        copy.wait()
+
+
+def last_part(mine_partial, part, theirs, even, odd, after):
+    rows, width = part.shape
+    return pl.pallas_call(
+        last_part_kernel,
+        in_specs=[VMEM] * 5 + [HBM],
+        out_specs=HBM,
+        out_shape=jax.ShapeDtypeStruct((rows, width), BF16),
+        scratch_shapes=[
+            pltpu.VMEM((rows, width), BF16),
+            pltpu.SemaphoreType.DMA((len(columns(width)),)),
+        ],
+        name="last_part",
+        **params(2 * even.shape[0] * rows * width, 8 * rows * width),
+    )(
+        *in_vmem(mine_partial, part, theirs, even, odd),
+        pltpu.with_memory_space_constraint(after, pltpu.HBM),
+    )
+
+
 def local(activations, out_grad, gate_weight, up_weight, down_weight):
     n_blk, n_tensor = lax.axis_size("blk"), lax.axis_size("tensor")
     hidden = gate_weight.shape[2]
@@ -361,20 +412,21 @@
         2 if pairs else 1,
     )
     back_early, back_late = [from_behind(t, "blk", -1) for t in (early, late)]
-    sums_early, sums_late = own_sums(activations, out_grad, own_hidden, own_grads, prev_gu)
-    total_down, total_gate = totals(sums_early, back_early, 2, hidden, activations)
+    sums_early, sums_late = own_sums(activations, out_grad, own_hidden, own_grads, back_early)
     if pairs:
         mine, sent = grads
         prev_other_even = lax.ppermute(prev_gu, axes, across)
         theirs = lax.ppermute(sent, "tensor", swap)
         other_gu = stack(other_gate, other_up, step, theirs)
         prev_other_odd = lax.ppermute(other_gu, axes, on_chip)
-        in_grad = in_grad_of(
-            total_gate,
-            ([mine], [[w_gu], [prev_gu]]),
-            ([theirs], [[other_gu], [prev_other_even, prev_other_odd]]),
+        mine_partial, part, done = ready_part(mine, w_gu, prev_gu, theirs, other_gu, sent)
+    else:
+        done = prev_gu
+    total_down, total_gate = totals(sums_early, back_early, 2, hidden, activations)
+    if pairs:
+        after = in_grad = last_part(
+            mine_partial, part, theirs, prev_other_even, prev_other_odd, total_gate
         )
-        after = in_grad
     else:
         after = in_grad_of(activations, (grads, [[w_gu], [prev_gu]]))
         in_grad = lax.psum_scatter(after, "tensor", scatter_dimension=0, tiled=True)

time: 53.3 us -> 52.6 us (0.987)
  waiting for transfers between devices: 17.3 us -> 16.2 us
    ppermute x1, waiting for transfers between devices: 1.48 us -> 0.67 us  [local(): prev_other_even = lax.ppermute(prev_gu, axes, across)]
    pallas_call x3 -> x4, Pallas kernels: 6.75 us -> 7.23 us  [the longest x2 3.71 us: totals(): pl.pallas_call(total_kernel, in_specs=[VMEM, VMEM, place], out_specs=[HBM...]
  transfers between devices with their start and end apart: 10 -> 10, of which waited for: 5 -> 5; matrix products, arithmetic and copies ran while one was open for 0% -> 0% of each run, Pallas kernels for 30% -> 32%
where the time goes in v2:
time: 52.6 us; the launch traced here: 52.4 us
  Pallas kernels  18 us (34%)
  waiting for transfers between devices  16.2 us (31%)
  starting transfers between devices  13.2 us (25%)
  local copies, waits for them, and re-layouts  4.24 us (8%)
  between operations  0.76 us (1%)
    ppermute x5, waiting for transfers between devices, from_behind(): lax.ppermute(value, axis, [(i, (i + by) % devices) for i in range(devices)])  14.3 us
    ppermute x5, starting transfers between devices, from_behind(): lax.ppermute(value, axis, [(i, (i + by) % devices) for i in range(devices)])  5.85 us
    pallas_call x1, Pallas kernels, own_meeting(): pl.pallas_call(own_kernel, in_specs=[VMEM] * 2 + [HBM] * 3, out_specs=[VM...  4.59 us
    unnamed x8, local copies, waits for them, and re-layouts  4.24 us
    pallas_call x2, Pallas kernels, totals(): pl.pallas_call(total_kernel, in_specs=[VMEM, VMEM, place], out_specs=[HBM...  3.71 us
    pallas_call x1, Pallas kernels, second_meeting(): pl.pallas_call(functools.partial(second_kernel, n_stacks, halves), in_spe...  3.36 us
    ppermute x2, starting transfers between devices, local(): lax.ppermute(w, 'tensor', swap)  2.03 us
    ppermute x1, starting transfers between devices, local(): theirs = lax.ppermute(sent, 'tensor', swap)  2 us
  transfers between devices with their start and end apart: 10, of which 5 were waited for; matrix products, arithmetic and copies ran while one was open for 0% of the time, Pallas kernels for 32%

profile of v2, /device:TPU:0, one launch (start us, length us, event | category | flops | bytes accessed | tf_op | source)
XLA Modules:
  0.0 52.4 jit_solution(5654924425375838085)
XLA Ops:
  0.6 0.5 collective-permute-start
  1.1 2.6 %collective-permute-start.1 = (bf16[54,5120]{1,0:T(8,128)(2,1)}, bf16[54,5120]{1,0:T(8,128)(2,1)S(1)}, u32[]{:S(2)}, u32[]{:S(2)}) collective-permute-start(bf16[54,5120]{1,0:T(8,128)(2,1)} %bitcast.15), channel_id=1, source_target_pairs={{0,2},{2,4},{4,6},{6,8},{8,10},{10,12},{12,14},{14,16},{16,18},{18... | collective-permute-start | bytes 1658888 | tf_op jit(solution)/shard_map/ppermute | solution.py:21
  3.8 0.1 collective-permute-start.2
  3.8 1.5 %collective-permute-start.4 = (bf16[54,5120]{1,0:T(8,128)(2,1)}, bf16[54,5120]{1,0:T(8,128)(2,1)S(1)}, u32[]{:S(2)}, u32[]{:S(2)}) collective-permute-start(bf16[54,5120]{1,0:T(8,128)(2,1)} %bitcast.16), channel_id=1, source_target_pairs={{0,1},{1,0},{2,3},{3,2},{4,5},{5,4},{6,7},{7,6},{8,9},{9,8},{10,11... | collective-permute-start | bytes 1658888 | tf_op jit(solution)/shard_map/ppermute | solution.py:401
  5.3 0.5 %collective-permute-start.5 = (bf16[54,5120]{1,0:T(8,128)(2,1)}, bf16[54,5120]{1,0:T(8,128)(2,1)S(1)}, u32[]{:S(2)}, u32[]{:S(2)}) collective-permute-start(bf16[54,5120]{1,0:T(8,128)(2,1)} %bitcast.19), channel_id=1, source_target_pairs={{0,1},{1,0},{2,3},{3,2},{4,5},{5,4},{6,7},{7,6},{8,9},{9,8},{10,11... | collective-permute-start | bytes 1658888 | tf_op jit(solution)/shard_map/ppermute | solution.py:401
  5.9 0.0 copy-start
  5.9 2.1 %copy-done = bf16[384,5120]{1,0:T(8,128)(2,1)S(1)} copy-done((bf16[384,5120]{1,0:T(8,128)(2,1)S(1)}, bf16[384,5120]{1,0:T(8,128)(2,1)}, u32[]{:S(2)}) %copy-start) | copy-done | bytes 3932184
  8.0 0.0 copy-start.2
  8.0 2.1 %copy-done.2 = bf16[384,5120]{1,0:T(8,128)(2,1)S(1)} copy-done((bf16[384,5120]{1,0:T(8,128)(2,1)S(1)}, bf16[384,5120]{1,0:T(8,128)(2,1)}, u32[]{:S(2)}) %copy-start.2) | copy-done | bytes 3932184
  10.1 0.0 copy-start.3
  10.1 4.6 %own_meeting.1 = (bf16[112,5120]{1,0:T(8,128)(2,1)S(1)}, bf16[112,384]{1,0:T(8,128)(2,1)S(1)}, bf16[56,384]{1,0:T(8,128)(2,1)S(1)}) custom-call(bf16[384,5120]{1,0:T(8,128)(2,1)S(1)} %copy-done, bf16[384,5120]{1,0:T(8,128)(2,1)S(1)} %copy-done.2, bf16[54,5120]{1,0:T(8,128)(2,1)} %bitcast.17, bf16[54,5120]{1,0:T(8,128)(2,1)} %bitcast.20, ...), custom_call_target="tpu_custom_call" | custom-call | flops 660602880 | bytes 7864320 | tf_op jit(solution)/shard_map/own_meeting/pallas_call | solution.py:125
  14.7 0.0 collective-permute-done.down_ref
  14.7 0.0 copy-done.3
  14.7 0.0 copy-start.1
  14.7 1.3 %grad_hidden.1.prev_ref = f32[54,384]{1,0:T(8,128)S(1)} custom-call(bf16[384,5120]{1,0:T(8,128)(2,1)S(1)} %copy-done.3, bf16[54,5120]{1,0:T(8,128)(2,1)S(1)} %collective-permute-done.down_ref, bf16[112,384]{1,0:T(8,128)(2,1)S(1)} %get-tuple-element.18.after_ref.own_ref.grads_ref), custom_call_target="tpu_custom_call" | custom-call | flops 212336640 | bytes 3932160 | tf_op jit(solution)/shard_map/grad_hidden/pallas_call | solution.py:147
  16.0 3.8 %collective-permute-done.1.refs_0_ = bf16[54,5120]{1,0:T(8,128)(2,1)S(1)} collective-permute-done((bf16[54,5120]{1,0:T(8,128)(2,1)}, bf16[54,5120]{1,0:T(8,128)(2,1)S(1)}, u32[]{:S(2)}, u32[]{:S(2)}) %collective-permute-start.1) | collective-permute-done | bytes 552992 | tf_op jit(solution)/shard_map/ppermute | solution.py:21
  19.9 6.1 %collective-permute-done.2.refs_1_ = bf16[54,5120]{1,0:T(8,128)(2,1)S(1)} collective-permute-done((bf16[54,5120]{1,0:T(8,128)(2,1)}, bf16[54,5120]{1,0:T(8,128)(2,1)S(1)}, u32[]{:S(2)}, u32[]{:S(2)}) %collective-permute-start.2) | collective-permute-done | bytes 552992 | tf_op jit(solution)/shard_map/ppermute | solution.py:21
  26.0 0.0 copy-done.1
  26.0 3.4 %second_meeting.1 = (bf16[112,5120]{1,0:T(8,128)(2,1)S(1)}, bf16[56,5120]{1,0:T(8,128)(2,1)S(1)}, bf16[112,5120]{1,0:T(8,128)(2,1)S(1)}, bf16[224,192]{1,0:T(8,128)(2,1)S(1)}, bf16[224,192]{1,0:T(8,128)(2,1)S(1)}) custom-call(bf16[384,5120]{1,0:T(8,128)(2,1)S(1)} %copy-done.1, bf16[384,5120]{1,0:T(8,128)(2,1)S(1)} %copy-done.3, ...), custom_call_target="tpu_custom_call" | custom-call | flops 1321205760 | bytes 7864320 | tf_op jit(solution)/shard_map/second_meeting/pallas_call | solution.py:190
  29.4 2.0 %collective-permute-start.3 = (bf16[224,192]{1,0:T(8,128)(2,1)S(1)}, bf16[224,192]{1,0:T(8,128)(2,1)S(1)}, u32[]{:S(2)}, u32[]{:S(2)}) collective-permute-start(bf16[224,192]{1,0:T(8,128)(2,1)S(1)} %get-tuple-element.22.after_ref), channel_id=1, source_target_pairs={{0,1},{1,0},{2,3},{3,2},{4,5},{5,4},{6,7},{7,6},{8,9},{9,8},{10,11... | collective-permute-start | bytes 258056 | tf_op jit(solution)/shard_map/ppermute | solution.py:419
  31.4 0.0 collective-permute-start.8
  31.4 2.0 %collective-permute-start.6 = (bf16[112,5120]{1,0:T(8,128)(2,1)S(1)}, bf16[112,5120]{1,0:T(8,128)(2,1)S(1)}, u32[]{:S(2)}, u32[]{:S(2)}) collective-permute-start(bf16[112,5120]{1,0:T(8,128)(2,1)S(1)} %get-tuple-element.21.prev_ref), channel_id=1, source_target_pairs={{0,1},{1,0},{4,5},{5,4},{8,9},{9,8},{12,13},{13,12},{16,17},{17,16... | collective-permute-start | bytes 3440648 | tf_op jit(solution)/shard_map/ppermute | solution.py:418
  33.4 0.0 collective-permute-done.4.gate_ref
  33.4 0.0 collective-permute-done.5.up_ref
  33.4 1.2 %collective-permute-done.3.after_ref.theirs_ref = bf16[224,192]{1,0:T(8,128)(2,1)S(1)} collective-permute-done((bf16[224,192]{1,0:T(8,128)(2,1)S(1)}, bf16[224,192]{1,0:T(8,128)(2,1)S(1)}, u32[]{:S(2)}, u32[]{:S(2)}) %collective-permute-start.3) | collective-permute-done | bytes 86048 | tf_op jit(solution)/shard_map/ppermute | solution.py:419
  34.6 0.1 stack.1.other_ref
  34.7 1.4 %collective-permute-start.7 = (bf16[112,5120]{1,0:T(8,128)(2,1)S(1)}, bf16[112,5120]{1,0:T(8,128)(2,1)S(1)}, u32[]{:S(2)}, u32[]{:S(2)}) collective-permute-start(bf16[112,5120]{1,0:T(8,128)(2,1)S(1)} %stack.1.other_ref), channel_id=1, source_target_pairs={{0,2},{1,3},{4,6},{5,7},{8,10},{9,11},{12,14},{13,15},{16,18},{17,... | collective-permute-start | bytes 3440648 | tf_op jit(solution)/shard_map/ppermute | solution.py:421
  36.1 2.6 %collective-permute-start.9 = (bf16[56,5120]{1,0:T(8,128)(2,1)S(1)}, bf16[56,5120]{1,0:T(8,128)(2,1)S(1)}, u32[]{:S(2)}, u32[]{:S(2)}) collective-permute-start(bf16[56,5120]{1,0:T(8,128)(2,1)S(1)} %get-tuple-element.30), channel_id=1, source_target_pairs={{0,30},{2,0},{4,2},{6,4},{8,6},{10,8},{12,10},{14,12},{16,14},{18,... | collective-permute-start | bytes 1720328 | tf_op jit(solution)/shard_map/ppermute | solution.py:21
  38.7 1.7 %ready_part.1 = (bf16[192,5120]{1,0:T(8,128)(2,1)S(1)}, f32[192,5120]{1,0:T(8,128)S(1)}, f32[8,128]{1,0:T(8,128)}) custom-call(bf16[224,192]{1,0:T(8,128)(2,1)S(1)} %get-tuple-element.19.mine_ref, bf16[112,5120]{1,0:T(8,128)(2,1)S(1)} %get-tuple-element.20.own_ref, bf16[112,5120]{1,0:T(8,128)(2,1)S(1)} %get-tuple-element.21.prev_ref, ...), custom_call_target="tpu_custom_call" | custom-call | flops 660602880 | bytes 5898240 | tf_op jit(solution)/shard_map/ready_part/pallas_call | solution.py:342
  40.5 4.3 %collective-permute-done.8.after_ref.back_ref = bf16[112,5120]{1,0:T(8,128)(2,1)S(1)} collective-permute-done((bf16[112,5120]{1,0:T(8,128)(2,1)S(1)}, bf16[112,5120]{1,0:T(8,128)(2,1)S(1)}, u32[]{:S(2)}, u32[]{:S(2)}) %collective-permute-start.8) | collective-permute-done | bytes 1146912 | tf_op jit(solution)/shard_map/ppermute | solution.py:21
  44.8 1.4 %own_sums.1 = (f32[112,5120]{1,0:T(8,128)S(1)}, f32[56,5120]{1,0:T(8,128)S(1)}) custom-call(bf16[384,5120]{1,0:T(8,128)(2,1)S(1)} %copy-done.1, bf16[384,5120]{1,0:T(8,128)(2,1)S(1)} %copy-done.3, bf16[56,384]{1,0:T(8,128)(2,1)S(1)} %get-tuple-element.25.hidden_ref, bf16[112,384]{1,0:T(8,128)(2,1)S(1)} %get-tuple-element.18.after_ref.own_ref.grads_ref, ...), custom_call_target="tpu_custom_call" | custom-call | flops 660602880 | bytes 7864320 | tf_op jit(solution)/shard_map/own_sums/pallas_call | solution.py:227
  46.2 2.3 %totals.2 = (f32[54,1,5120]{2,1,0:T(1,128)}, f32[54,1,5120]{2,1,0:T(1,128)}) custom-call(f32[112,5120]{1,0:T(8,128)S(1)} %get-tuple-element.27.own_ref, bf16[112,5120]{1,0:T(8,128)(2,1)S(1)} %collective-permute-done.8.after_ref.back_ref, bf16[384,5120]{1,0:T(8,128)(2,1)} %after_ref.1), custom_call_target="tpu_custom_call" | custom-call | flops 573440 | bytes 5734400 | tf_op jit(solution)/shard_map/totals/pallas_call | solution.py:256
  48.5 0.7 %collective-permute-done.6.even_ref = bf16[112,5120]{1,0:T(8,128)(2,1)S(1)} collective-permute-done((bf16[112,5120]{1,0:T(8,128)(2,1)S(1)}, bf16[112,5120]{1,0:T(8,128)(2,1)S(1)}, u32[]{:S(2)}, u32[]{:S(2)}) %collective-permute-start.6) | collective-permute-done | bytes 1146912 | tf_op jit(solution)/shard_map/ppermute | solution.py:418
  49.1 0.0 collective-permute-done.7.odd_ref
  49.1 1.8 %last_part.1.after_ref = bf16[192,5120]{1,0:T(8,128)(2,1)} custom-call(bf16[192,5120]{1,0:T(8,128)(2,1)S(1)} %get-tuple-element.23.mine_ref, f32[192,5120]{1,0:T(8,128)S(1)} %get-tuple-element.24.part_ref, bf16[224,192]{1,0:T(8,128)(2,1)S(1)} %collective-permute-done.3.after_ref.theirs_ref, bf16[112,5120]{1,0:T(8,128)(2,1)S(1)} %collective-permute-done.6.even_ref, ...), custom_call_target="tpu_custom_call" | custom-call | flops 220200960 | bytes 7864320 | tf_op jit(solution)/shard_map/last_part/pallas_call | solution.py:371
  51.0 0.0 collective-permute-done.9.back_ref
  51.0 1.4 %totals.3 = f32[54,1,5120]{2,1,0:T(1,128)} custom-call(f32[56,5120]{1,0:T(8,128)S(1)} %get-tuple-element.29.own_ref, bf16[56,5120]{1,0:T(8,128)(2,1)S(1)} %collective-permute-done.9.back_ref, bf16[192,5120]{1,0:T(8,128)(2,1)} %last_part.1.after_ref), custom_call_target="tpu_custom_call" | custom-call | flops 286720 | bytes 2867200 | tf_op jit(solution)/shard_map/totals/pallas_call | solution.py:256
Async XLA Ops:
  0.6 14.1 %collective-permute-start = (bf16[54,5120]{1,0:T(8,128)(2,1)}, bf16[54,5120]{1,0:T(8,128)(2,1)S(1)}, u32[]{:S(2)}, u32[]{:S(2)}) collective-permute-start(bf16[54,5120]{1,0:T(8,128)(2,1)} %bitcast.13), channel_id=1, source_target_pairs={{0,2},{2,4},{4,6},{6,8},{8,10},{10,12},{12,14},{14,16},{16,18},{18... | collective-permute-start | bytes 1658888 | tf_op jit(solution)/shard_map/ppermute | solution.py:21
  1.1 18.7 %collective-permute-start.1 = (bf16[54,5120]{1,0:T(8,128)(2,1)}, bf16[54,5120]{1,0:T(8,128)(2,1)S(1)}, u32[]{:S(2)}, u32[]{:S(2)}) collective-permute-start(bf16[54,5120]{1,0:T(8,128)(2,1)} %bitcast.15), channel_id=1, source_target_pairs={{0,2},{2,4},{4,6},{6,8},{8,10},{10,12},{12,14},{14,16},{16,18},{18... | collective-permute-start | bytes 1658888 | tf_op jit(solution)/shard_map/ppermute | solution.py:21
  3.8 22.3 %collective-permute-start.2 = (bf16[54,5120]{1,0:T(8,128)(2,1)}, bf16[54,5120]{1,0:T(8,128)(2,1)S(1)}, u32[]{:S(2)}, u32[]{:S(2)}) collective-permute-start(bf16[54,5120]{1,0:T(8,128)(2,1)} %bitcast.18), channel_id=1, source_target_pairs={{0,2},{2,4},{4,6},{6,8},{8,10},{10,12},{12,14},{14,16},{16,18},{18... | collective-permute-start | bytes 1658888 | tf_op jit(solution)/shard_map/ppermute | solution.py:21
  3.8 29.6 %collective-permute-start.4 = (bf16[54,5120]{1,0:T(8,128)(2,1)}, bf16[54,5120]{1,0:T(8,128)(2,1)S(1)}, u32[]{:S(2)}, u32[]{:S(2)}) collective-permute-start(bf16[54,5120]{1,0:T(8,128)(2,1)} %bitcast.16), channel_id=1, source_target_pairs={{0,1},{1,0},{2,3},{3,2},{4,5},{5,4},{6,7},{7,6},{8,9},{9,8},{10,11... | collective-permute-start | bytes 1658888 | tf_op jit(solution)/shard_map/ppermute | solution.py:401
  5.3 28.1 %collective-permute-start.5 = (bf16[54,5120]{1,0:T(8,128)(2,1)}, bf16[54,5120]{1,0:T(8,128)(2,1)S(1)}, u32[]{:S(2)}, u32[]{:S(2)}) collective-permute-start(bf16[54,5120]{1,0:T(8,128)(2,1)} %bitcast.19), channel_id=1, source_target_pairs={{0,1},{1,0},{2,3},{3,2},{4,5},{5,4},{6,7},{7,6},{8,9},{9,8},{10,11... | collective-permute-start | bytes 1658888 | tf_op jit(solution)/shard_map/ppermute | solution.py:401
  5.9 2.1 %copy-start = (bf16[384,5120]{1,0:T(8,128)(2,1)S(1)}, bf16[384,5120]{1,0:T(8,128)(2,1)}, u32[]{:S(2)}) copy-start(bf16[384,5120]{1,0:T(8,128)(2,1)} %after_ref.1) | copy-start | bytes 11796484
  8.0 2.1 %copy-start.2 = (bf16[384,5120]{1,0:T(8,128)(2,1)S(1)}, bf16[384,5120]{1,0:T(8,128)(2,1)}, u32[]{:S(2)}) copy-start(bf16[384,5120]{1,0:T(8,128)(2,1)} %g_ref.7) | copy-start | bytes 11796484
  10.1 4.6 %copy-start.3 = (bf16[384,5120]{1,0:T(8,128)(2,1)S(1)}, bf16[384,5120]{1,0:T(8,128)(2,1)}, u32[]{:S(2)}) copy-start(bf16[384,5120]{1,0:T(8,128)(2,1)} %g_ref.7) | copy-start | bytes 11796484
  14.7 11.3 %copy-start.1 = (bf16[384,5120]{1,0:T(8,128)(2,1)S(1)}, bf16[384,5120]{1,0:T(8,128)(2,1)}, u32[]{:S(2)}) copy-start(bf16[384,5120]{1,0:T(8,128)(2,1)} %after_ref.1) | copy-start | bytes 11796484
  29.4 5.3 %collective-permute-start.3 = (bf16[224,192]{1,0:T(8,128)(2,1)S(1)}, bf16[224,192]{1,0:T(8,128)(2,1)S(1)}, u32[]{:S(2)}, u32[]{:S(2)}) collective-permute-start(bf16[224,192]{1,0:T(8,128)(2,1)S(1)} %get-tuple-element.22.after_ref), channel_id=1, source_target_pairs={{0,1},{1,0},{2,3},{3,2},{4,5},{5,4},{6,7},{7,6},{8,9},{9,8},{10,11... | collective-permute-start | bytes 258056 | tf_op jit(solution)/shard_map/ppermute | solution.py:419
  31.4 13.4 %collective-permute-start.8 = (bf16[112,5120]{1,0:T(8,128)(2,1)S(1)}, bf16[112,5120]{1,0:T(8,128)(2,1)S(1)}, u32[]{:S(2)}, u32[]{:S(2)}) collective-permute-start(bf16[112,5120]{1,0:T(8,128)(2,1)S(1)} %get-tuple-element.26), channel_id=1, source_target_pairs={{0,30},{2,0},{4,2},{6,4},{8,6},{10,8},{12,10},{14,12},{16,14},{18,... | collective-permute-start | bytes 3440648 | tf_op jit(solution)/shard_map/ppermute | solution.py:21
  31.4 17.7 %collective-permute-start.6 = (bf16[112,5120]{1,0:T(8,128)(2,1)S(1)}, bf16[112,5120]{1,0:T(8,128)(2,1)S(1)}, u32[]{:S(2)}, u32[]{:S(2)}) collective-permute-start(bf16[112,5120]{1,0:T(8,128)(2,1)S(1)} %get-tuple-element.21.prev_ref), channel_id=1, source_target_pairs={{0,1},{1,0},{4,5},{5,4},{8,9},{9,8},{12,13},{13,12},{16,17},{17,16... | collective-permute-start | bytes 3440648 | tf_op jit(solution)/shard_map/ppermute | solution.py:418
  34.7 14.4 %collective-permute-start.7 = (bf16[112,5120]{1,0:T(8,128)(2,1)S(1)}, bf16[112,5120]{1,0:T(8,128)(2,1)S(1)}, u32[]{:S(2)}, u32[]{:S(2)}) collective-permute-start(bf16[112,5120]{1,0:T(8,128)(2,1)S(1)} %stack.1.other_ref), channel_id=1, source_target_pairs={{0,2},{1,3},{4,6},{5,7},{8,10},{9,11},{12,14},{13,15},{16,18},{17,... | collective-permute-start | bytes 3440648 | tf_op jit(solution)/shard_map/ppermute | solution.py:421
  36.1 14.9 %collective-permute-start.9 = (bf16[56,5120]{1,0:T(8,128)(2,1)S(1)}, bf16[56,5120]{1,0:T(8,128)(2,1)S(1)}, u32[]{:S(2)}, u32[]{:S(2)}) collective-permute-start(bf16[56,5120]{1,0:T(8,128)(2,1)S(1)} %get-tuple-element.30), channel_id=1, source_target_pairs={{0,30},{2,0},{4,2},{6,4},{8,6},{10,8},{12,10},{14,12},{16,14},{18,... | collective-permute-start | bytes 1720328 | tf_op jit(solution)/shard_map/ppermute | solution.py:21

commit v3 on v2

--- a/solution.py
+++ b/solution.py
@@ -353,9 +353,21 @@
     )(*in_vmem(mine, own, prev, theirs, other), after)
 
 
-def last_part_kernel(mine_ref, part_ref, theirs_ref, even_ref, odd_ref, after_ref, out_ref, scratch, sem):
-    del after_ref
-    stores = []
+def add_rows(total_ref, own_ref, back_ref, first_row, out_ref, sem):
+    hidden, stores = out_ref.shape[0], []
+    for first in range(0, hidden, 8):
+        part = pl.ds(first_row + first, 8)
+        total_ref[part, :] = own_ref[part, :] + back_ref[part, :].astype(F32)
+        for r in range(first, min(first + 8, hidden)):
+            row = total_ref.at[pl.ds(first_row + r, 1), :]
+            stores.append(pltpu.make_async_copy(row, out_ref.at[r], sem.at[r]))
+            stores[-1].start()
+    return stores
+
+
+def last_kernel(mine_ref, part_ref, theirs_ref, even_ref, odd_ref, own_ref, back_ref, after_ref, out_ref, up_ref, scratch, total_ref, sem, up_sem):
+    del after_ref
+    stores = add_rows(total_ref, own_ref, back_ref, 0, up_ref, up_sem)
     for n, at in enumerate(columns(out_ref.shape[1])):
         term = dot_left(theirs_ref[even_ref.shape[0] :, :], even_ref[:, at] + odd_ref[:, at])
         theirs = (part_ref[:, at] + term).astype(BF16)
@@ -366,21 +378,26 @@
         copy.wait()
 
 
-def last_part(mine_partial, part, theirs, even, odd, after):
+def last_part(mine_partial, part, theirs, even, odd, own, back, hidden, after):
     rows, width = part.shape
     return pl.pallas_call(
-        last_part_kernel,
-        in_specs=[VMEM] * 5 + [HBM],
-        out_specs=HBM,
-        out_shape=jax.ShapeDtypeStruct((rows, width), BF16),
+        last_kernel,
+        in_specs=[VMEM] * 7 + [HBM],
+        out_specs=[HBM] * 2,
+        out_shape=[
+            jax.ShapeDtypeStruct((rows, width), BF16),
+            jax.ShapeDtypeStruct((hidden, 1, width), F32),
+        ],
         scratch_shapes=[
             pltpu.VMEM((rows, width), BF16),
+            pltpu.VMEM(own.shape, F32),
             pltpu.SemaphoreType.DMA((len(columns(width)),)),
+            pltpu.SemaphoreType.DMA((hidden,)),
         ],
         name="last_part",
         **params(2 * even.shape[0] * rows * width, 8 * rows * width),
     )(
-        *in_vmem(mine_partial, part, theirs, even, odd),
+        *in_vmem(mine_partial, part, theirs, even, odd, own, back),
         pltpu.with_memory_space_constraint(after, pltpu.HBM),
     )
 
@@ -419,18 +436,26 @@
         theirs = lax.ppermute(sent, "tensor", swap)
         other_gu = stack(other_gate, other_up, step, theirs)
         prev_other_odd = lax.ppermute(other_gu, axes, on_chip)
-        mine_partial, part, done = ready_part(mine, w_gu, prev_gu, theirs, other_gu, sent)
+        mine_partial, part, done = ready_part(mine, w_gu, prev_gu, theirs, other_gu, sums_late)
     else:
         done = prev_gu
     total_down, total_gate = totals(sums_early, back_early, 2, hidden, activations)
     if pairs:
-        after = in_grad = last_part(
-            mine_partial, part, theirs, prev_other_even, prev_other_odd, total_gate
+        in_grad, total_up = last_part(
+            mine_partial,
+            part,
+            theirs,
+            prev_other_even,
+            prev_other_odd,
+            sums_late,
+            back_late,
+            hidden,
+            total_gate,
         )
     else:
         after = in_grad_of(activations, (grads, [[w_gu], [prev_gu]]))
         in_grad = lax.psum_scatter(after, "tensor", scatter_dimension=0, tiled=True)
-    [total_up] = totals(sums_late, back_late, 1, hidden, after)
+        [total_up] = totals(sums_late, back_late, 1, hidden, after)
     return (
         in_grad,
         total_gate.transpose(1, 2, 0),

time: 52.6 us -> 52.1 us (level)
  Pallas kernels: 18 us -> 17.4 us
  waiting for transfers between devices: 16.2 us -> 16.8 us
    pallas_call x2 -> x1, Pallas kernels: 3.71 us -> 2.27 us  [totals(): pl.pallas_call(total_kernel, in_specs=[VMEM, VMEM, place], out_specs=[HBM...]
    ppermute x5, starting transfers between devices: 5.85 us -> 4.89 us  [from_behind(): lax.ppermute(value, axis, [(i, (i + by) % devices) for i in range(devices)])]
    pallas_call x1, Pallas kernels: 1.81 us -> 2.63 us  [last_part(): pl.pallas_call(last_kernel, in_specs=[VMEM] * 7 + [HBM], out_specs=[HBM]...]
    ppermute x5, waiting for transfers between devices: 14.3 us -> 14.9 us  [from_behind(): lax.ppermute(value, axis, [(i, (i + by) % devices) for i in range(devices)])]
  transfers between devices with their start and end apart: 10 -> 10, of which waited for: 5 -> 6; matrix products, arithmetic and copies ran while one was open for 0% -> 0% of each run, Pallas kernels for 32% -> 28%
where the time goes in v3:
time: 52.1 us; the launch traced here: 51.8 us
  Pallas kernels  17.4 us (33%)
  waiting for transfers between devices  16.8 us (32%)
  starting transfers between devices  12.7 us (24%)
  local copies, waits for them, and re-layouts  4.24 us (8%)
  between operations  0.75 us (1%)
    ppermute x5, waiting for transfers between devices, from_behind(): lax.ppermute(value, axis, [(i, (i + by) % devices) for i in range(devices)])  14.9 us
    ppermute x5, starting transfers between devices, from_behind(): lax.ppermute(value, axis, [(i, (i + by) % devices) for i in range(devices)])  4.89 us
    pallas_call x1, Pallas kernels, own_meeting(): pl.pallas_call(own_kernel, in_specs=[VMEM] * 2 + [HBM] * 3, out_specs=[VM...  4.59 us
    unnamed x8, local copies, waits for them, and re-layouts  4.24 us
    pallas_call x1, Pallas kernels, second_meeting(): pl.pallas_call(functools.partial(second_kernel, n_stacks, halves), in_spe...  3.36 us
    pallas_call x1, Pallas kernels, last_part(): pl.pallas_call(last_kernel, in_specs=[VMEM] * 7 + [HBM], out_specs=[HBM]...  2.63 us
    pallas_call x1, Pallas kernels, totals(): pl.pallas_call(total_kernel, in_specs=[VMEM, VMEM, place], out_specs=[HBM...  2.27 us
    ppermute x2, starting transfers between devices, local(): lax.ppermute(w, 'tensor', swap)  2.03 us
  transfers between devices with their start and end apart: 10, of which 6 were waited for; matrix products, arithmetic and copies ran while one was open for 0% of the time, Pallas kernels for 28%

profile of v3, /device:TPU:0, one launch (start us, length us, event | category | flops | bytes accessed | tf_op | source)
XLA Modules:
  0.0 51.8 jit_solution(10833782088632318912)
XLA Ops:
  0.6 0.5 collective-permute-start
  1.1 2.6 %collective-permute-start.1 = (bf16[54,5120]{1,0:T(8,128)(2,1)}, bf16[54,5120]{1,0:T(8,128)(2,1)S(1)}, u32[]{:S(2)}, u32[]{:S(2)}) collective-permute-start(bf16[54,5120]{1,0:T(8,128)(2,1)} %bitcast.14), channel_id=1, source_target_pairs={{0,2},{2,4},{4,6},{6,8},{8,10},{10,12},{12,14},{14,16},{16,18},{18... | collective-permute-start | bytes 1658888 | tf_op jit(solution)/shard_map/ppermute | solution.py:21
  3.8 0.1 collective-permute-start.2
  3.8 1.5 %collective-permute-start.4 = (bf16[54,5120]{1,0:T(8,128)(2,1)}, bf16[54,5120]{1,0:T(8,128)(2,1)S(1)}, u32[]{:S(2)}, u32[]{:S(2)}) collective-permute-start(bf16[54,5120]{1,0:T(8,128)(2,1)} %bitcast.15), channel_id=1, source_target_pairs={{0,1},{1,0},{2,3},{3,2},{4,5},{5,4},{6,7},{7,6},{8,9},{9,8},{10,11... | collective-permute-start | bytes 1658888 | tf_op jit(solution)/shard_map/ppermute | solution.py:418
  5.3 0.5 %collective-permute-start.5 = (bf16[54,5120]{1,0:T(8,128)(2,1)}, bf16[54,5120]{1,0:T(8,128)(2,1)S(1)}, u32[]{:S(2)}, u32[]{:S(2)}) collective-permute-start(bf16[54,5120]{1,0:T(8,128)(2,1)} %bitcast.18), channel_id=1, source_target_pairs={{0,1},{1,0},{2,3},{3,2},{4,5},{5,4},{6,7},{7,6},{8,9},{9,8},{10,11... | collective-permute-start | bytes 1658888 | tf_op jit(solution)/shard_map/ppermute | solution.py:418
  5.9 0.0 copy-start
  5.9 2.1 %copy-done = bf16[384,5120]{1,0:T(8,128)(2,1)S(1)} copy-done((bf16[384,5120]{1,0:T(8,128)(2,1)S(1)}, bf16[384,5120]{1,0:T(8,128)(2,1)}, u32[]{:S(2)}) %copy-start) | copy-done | bytes 3932184
  8.0 0.0 copy-start.2
  8.0 2.1 %copy-done.2 = bf16[384,5120]{1,0:T(8,128)(2,1)S(1)} copy-done((bf16[384,5120]{1,0:T(8,128)(2,1)S(1)}, bf16[384,5120]{1,0:T(8,128)(2,1)}, u32[]{:S(2)}) %copy-start.2) | copy-done | bytes 3932184
  10.1 0.0 copy-start.3
  10.1 4.6 %own_meeting.1 = (bf16[112,5120]{1,0:T(8,128)(2,1)S(1)}, bf16[112,384]{1,0:T(8,128)(2,1)S(1)}, bf16[56,384]{1,0:T(8,128)(2,1)S(1)}) custom-call(bf16[384,5120]{1,0:T(8,128)(2,1)S(1)} %copy-done, bf16[384,5120]{1,0:T(8,128)(2,1)S(1)} %copy-done.2, bf16[54,5120]{1,0:T(8,128)(2,1)} %bitcast.16, bf16[54,5120]{1,0:T(8,128)(2,1)} %bitcast.19, ...), custom_call_target="tpu_custom_call" | custom-call | flops 660602880 | bytes 7864320 | tf_op jit(solution)/shard_map/own_meeting/pallas_call | solution.py:125
  14.7 0.0 collective-permute-done.down_ref
  14.7 0.0 copy-done.3
  14.7 0.0 copy-start.1
  14.7 1.3 %grad_hidden.1.prev_ref = f32[54,384]{1,0:T(8,128)S(1)} custom-call(bf16[384,5120]{1,0:T(8,128)(2,1)S(1)} %copy-done.3, bf16[54,5120]{1,0:T(8,128)(2,1)S(1)} %collective-permute-done.down_ref, bf16[112,384]{1,0:T(8,128)(2,1)S(1)} %get-tuple-element.20.after_ref.own_ref.grads_ref), custom_call_target="tpu_custom_call" | custom-call | flops 212336640 | bytes 3932160 | tf_op jit(solution)/shard_map/grad_hidden/pallas_call | solution.py:147
  16.0 3.8 %collective-permute-done.1.refs_0_ = bf16[54,5120]{1,0:T(8,128)(2,1)S(1)} collective-permute-done((bf16[54,5120]{1,0:T(8,128)(2,1)}, bf16[54,5120]{1,0:T(8,128)(2,1)S(1)}, u32[]{:S(2)}, u32[]{:S(2)}) %collective-permute-start.1) | collective-permute-done | bytes 552992 | tf_op jit(solution)/shard_map/ppermute | solution.py:21
  19.9 6.1 %collective-permute-done.2.refs_1_ = bf16[54,5120]{1,0:T(8,128)(2,1)S(1)} collective-permute-done((bf16[54,5120]{1,0:T(8,128)(2,1)}, bf16[54,5120]{1,0:T(8,128)(2,1)S(1)}, u32[]{:S(2)}, u32[]{:S(2)}) %collective-permute-start.2) | collective-permute-done | bytes 552992 | tf_op jit(solution)/shard_map/ppermute | solution.py:21
  26.0 0.0 copy-done.1
  26.0 3.4 %second_meeting.1 = (bf16[112,5120]{1,0:T(8,128)(2,1)S(1)}, bf16[56,5120]{1,0:T(8,128)(2,1)S(1)}, bf16[112,5120]{1,0:T(8,128)(2,1)S(1)}, bf16[224,192]{1,0:T(8,128)(2,1)S(1)}, bf16[224,192]{1,0:T(8,128)(2,1)S(1)}) custom-call(bf16[384,5120]{1,0:T(8,128)(2,1)S(1)} %copy-done.1, bf16[384,5120]{1,0:T(8,128)(2,1)S(1)} %copy-done.3, ...), custom_call_target="tpu_custom_call" | custom-call | flops 1321205760 | bytes 7864320 | tf_op jit(solution)/shard_map/second_meeting/pallas_call | solution.py:190
  29.4 0.1 collective-permute-start.6
  29.5 2.0 %collective-permute-start.3 = (bf16[224,192]{1,0:T(8,128)(2,1)S(1)}, bf16[224,192]{1,0:T(8,128)(2,1)S(1)}, u32[]{:S(2)}, u32[]{:S(2)}) collective-permute-start(bf16[224,192]{1,0:T(8,128)(2,1)S(1)} %get-tuple-element.24), channel_id=1, source_target_pairs={{0,1},{1,0},{2,3},{3,2},{4,5},{5,4},{6,7},{7,6},{8,9},{9,8},{10,11... | collective-permute-start | bytes 258056 | tf_op jit(solution)/shard_map/ppermute | solution.py:436
  31.5 2.0 %collective-permute-start.7 = (bf16[112,5120]{1,0:T(8,128)(2,1)S(1)}, bf16[112,5120]{1,0:T(8,128)(2,1)S(1)}, u32[]{:S(2)}, u32[]{:S(2)}) collective-permute-start(bf16[112,5120]{1,0:T(8,128)(2,1)S(1)} %get-tuple-element.23.prev_ref), channel_id=1, source_target_pairs={{0,1},{1,0},{4,5},{5,4},{8,9},{9,8},{12,13},{13,12},{16,17},{17,16... | collective-permute-start | bytes 3440648 | tf_op jit(solution)/shard_map/ppermute | solution.py:435
  33.5 0.0 collective-permute-done.4.gate_ref
  33.5 0.0 collective-permute-done.5.up_ref
  33.5 1.7 %collective-permute-done.3.after_ref.theirs_ref = bf16[224,192]{1,0:T(8,128)(2,1)S(1)} collective-permute-done((bf16[224,192]{1,0:T(8,128)(2,1)S(1)}, bf16[224,192]{1,0:T(8,128)(2,1)S(1)}, u32[]{:S(2)}, u32[]{:S(2)}) %collective-permute-start.3) | collective-permute-done | bytes 86048 | tf_op jit(solution)/shard_map/ppermute | solution.py:436
  35.2 0.1 stack.1.other_ref
  35.3 1.7 %collective-permute-start.8 = (bf16[112,5120]{1,0:T(8,128)(2,1)S(1)}, bf16[112,5120]{1,0:T(8,128)(2,1)S(1)}, u32[]{:S(2)}, u32[]{:S(2)}) collective-permute-start(bf16[112,5120]{1,0:T(8,128)(2,1)S(1)} %stack.1.other_ref), channel_id=1, source_target_pairs={{0,2},{1,3},{4,6},{5,7},{8,10},{9,11},{12,14},{13,15},{16,18},{17,... | collective-permute-start | bytes 3440648 | tf_op jit(solution)/shard_map/ppermute | solution.py:438
  37.0 1.6 %collective-permute-start.9 = (bf16[56,5120]{1,0:T(8,128)(2,1)S(1)}, bf16[56,5120]{1,0:T(8,128)(2,1)S(1)}, u32[]{:S(2)}, u32[]{:S(2)}) collective-permute-start(bf16[56,5120]{1,0:T(8,128)(2,1)S(1)} %get-tuple-element.30), channel_id=1, source_target_pairs={{0,30},{2,0},{4,2},{6,4},{8,6},{10,8},{12,10},{14,12},{16,14},{18,... | collective-permute-start | bytes 1720328 | tf_op jit(solution)/shard_map/ppermute | solution.py:21
  38.7 4.1 %collective-permute-done.6.after_ref.back_ref = bf16[112,5120]{1,0:T(8,128)(2,1)S(1)} collective-permute-done((bf16[112,5120]{1,0:T(8,128)(2,1)S(1)}, bf16[112,5120]{1,0:T(8,128)(2,1)S(1)}, u32[]{:S(2)}, u32[]{:S(2)}) %collective-permute-start.6) | collective-permute-done | bytes 1146912 | tf_op jit(solution)/shard_map/ppermute | solution.py:21
  42.8 1.4 %own_sums.1 = (f32[112,5120]{1,0:T(8,128)S(1)}, f32[56,5120]{1,0:T(8,128)S(1)}) custom-call(bf16[384,5120]{1,0:T(8,128)(2,1)S(1)} %copy-done.1, bf16[384,5120]{1,0:T(8,128)(2,1)S(1)} %copy-done.3, bf16[56,384]{1,0:T(8,128)(2,1)S(1)} %get-tuple-element.25.hidden_ref, bf16[112,384]{1,0:T(8,128)(2,1)S(1)} %get-tuple-element.20.after_ref.own_ref.grads_ref, ...), custom_call_target="tpu_custom_call" | custom-call | flops 660602880 | bytes 7864320 | tf_op jit(solution)/shard_map/own_sums/pallas_call | solution.py:227
  44.2 2.3 %totals.1 = (f32[54,1,5120]{2,1,0:T(1,128)}, f32[54,1,5120]{2,1,0:T(1,128)}) custom-call(f32[112,5120]{1,0:T(8,128)S(1)} %get-tuple-element.31.own_ref, bf16[112,5120]{1,0:T(8,128)(2,1)S(1)} %collective-permute-done.6.after_ref.back_ref, bf16[384,5120]{1,0:T(8,128)(2,1)} %after_ref.1), custom_call_target="tpu_custom_call" | custom-call | flops 573440 | bytes 5734400 | tf_op jit(solution)/shard_map/totals/pallas_call | solution.py:256
  46.5 1.7 %ready_part.1 = (bf16[192,5120]{1,0:T(8,128)(2,1)S(1)}, f32[192,5120]{1,0:T(8,128)S(1)}, f32[8,128]{1,0:T(8,128)}) custom-call(bf16[224,192]{1,0:T(8,128)(2,1)S(1)} %get-tuple-element.21.mine_ref, bf16[112,5120]{1,0:T(8,128)(2,1)S(1)} %get-tuple-element.22.own_ref, bf16[112,5120]{1,0:T(8,128)(2,1)S(1)} %get-tuple-element.23.prev_ref, ...), custom_call_target="tpu_custom_call" | custom-call | flops 660602880 | bytes 5898240 | tf_op jit(solution)/shard_map/ready_part/pallas_call | solution.py:342
  48.2 0.7 %collective-permute-done.9.back_ref = bf16[56,5120]{1,0:T(8,128)(2,1)S(1)} collective-permute-done((bf16[56,5120]{1,0:T(8,128)(2,1)S(1)}, bf16[56,5120]{1,0:T(8,128)(2,1)S(1)}, u32[]{:S(2)}, u32[]{:S(2)}) %collective-permute-start.9) | collective-permute-done | bytes 573472 | tf_op jit(solution)/shard_map/ppermute | solution.py:21
  49.0 0.2 collective-permute-done.7.even_ref
  49.2 0.0 collective-permute-done.8.odd_ref
  49.2 2.6 %last_part.1 = (bf16[192,5120]{1,0:T(8,128)(2,1)}, f32[54,1,5120]{2,1,0:T(1,128)}) custom-call(bf16[192,5120]{1,0:T(8,128)(2,1)S(1)} %get-tuple-element.28.mine_ref, f32[192,5120]{1,0:T(8,128)S(1)} %get-tuple-element.29.part_ref, bf16[224,192]{1,0:T(8,128)(2,1)S(1)} %collective-permute-done.3.after_ref.theirs_ref, ...), custom_call_target="tpu_custom_call" | custom-call | flops 220200960 | bytes 7864320 | tf_op jit(solution)/shard_map/last_part/pallas_call | solution.py:383
Async XLA Ops:
  0.6 14.1 %collective-permute-start = (bf16[54,5120]{1,0:T(8,128)(2,1)}, bf16[54,5120]{1,0:T(8,128)(2,1)S(1)}, u32[]{:S(2)}, u32[]{:S(2)}) collective-permute-start(bf16[54,5120]{1,0:T(8,128)(2,1)} %bitcast.12), channel_id=1, source_target_pairs={{0,2},{2,4},{4,6},{6,8},{8,10},{10,12},{12,14},{14,16},{16,18},{18... | collective-permute-start | bytes 1658888 | tf_op jit(solution)/shard_map/ppermute | solution.py:21
  1.1 18.7 %collective-permute-start.1 = (bf16[54,5120]{1,0:T(8,128)(2,1)}, bf16[54,5120]{1,0:T(8,128)(2,1)S(1)}, u32[]{:S(2)}, u32[]{:S(2)}) collective-permute-start(bf16[54,5120]{1,0:T(8,128)(2,1)} %bitcast.14), channel_id=1, source_target_pairs={{0,2},{2,4},{4,6},{6,8},{8,10},{10,12},{12,14},{14,16},{16,18},{18... | collective-permute-start | bytes 1658888 | tf_op jit(solution)/shard_map/ppermute | solution.py:21
  3.8 22.3 %collective-permute-start.2 = (bf16[54,5120]{1,0:T(8,128)(2,1)}, bf16[54,5120]{1,0:T(8,128)(2,1)S(1)}, u32[]{:S(2)}, u32[]{:S(2)}) collective-permute-start(bf16[54,5120]{1,0:T(8,128)(2,1)} %bitcast.17), channel_id=1, source_target_pairs={{0,2},{2,4},{4,6},{6,8},{8,10},{10,12},{12,14},{14,16},{16,18},{18... | collective-permute-start | bytes 1658888 | tf_op jit(solution)/shard_map/ppermute | solution.py:21
  3.8 29.6 %collective-permute-start.4 = (bf16[54,5120]{1,0:T(8,128)(2,1)}, bf16[54,5120]{1,0:T(8,128)(2,1)S(1)}, u32[]{:S(2)}, u32[]{:S(2)}) collective-permute-start(bf16[54,5120]{1,0:T(8,128)(2,1)} %bitcast.15), channel_id=1, source_target_pairs={{0,1},{1,0},{2,3},{3,2},{4,5},{5,4},{6,7},{7,6},{8,9},{9,8},{10,11... | collective-permute-start | bytes 1658888 | tf_op jit(solution)/shard_map/ppermute | solution.py:418
  5.3 28.1 %collective-permute-start.5 = (bf16[54,5120]{1,0:T(8,128)(2,1)}, bf16[54,5120]{1,0:T(8,128)(2,1)S(1)}, u32[]{:S(2)}, u32[]{:S(2)}) collective-permute-start(bf16[54,5120]{1,0:T(8,128)(2,1)} %bitcast.18), channel_id=1, source_target_pairs={{0,1},{1,0},{2,3},{3,2},{4,5},{5,4},{6,7},{7,6},{8,9},{9,8},{10,11... | collective-permute-start | bytes 1658888 | tf_op jit(solution)/shard_map/ppermute | solution.py:418
  5.9 2.1 %copy-start = (bf16[384,5120]{1,0:T(8,128)(2,1)S(1)}, bf16[384,5120]{1,0:T(8,128)(2,1)}, u32[]{:S(2)}) copy-start(bf16[384,5120]{1,0:T(8,128)(2,1)} %after_ref.1) | copy-start | bytes 11796484
  8.0 2.1 %copy-start.2 = (bf16[384,5120]{1,0:T(8,128)(2,1)S(1)}, bf16[384,5120]{1,0:T(8,128)(2,1)}, u32[]{:S(2)}) copy-start(bf16[384,5120]{1,0:T(8,128)(2,1)} %g_ref.7) | copy-start | bytes 11796484
  10.1 4.6 %copy-start.3 = (bf16[384,5120]{1,0:T(8,128)(2,1)S(1)}, bf16[384,5120]{1,0:T(8,128)(2,1)}, u32[]{:S(2)}) copy-start(bf16[384,5120]{1,0:T(8,128)(2,1)} %g_ref.7) | copy-start | bytes 11796484
  14.7 11.3 %copy-start.1 = (bf16[384,5120]{1,0:T(8,128)(2,1)S(1)}, bf16[384,5120]{1,0:T(8,128)(2,1)}, u32[]{:S(2)}) copy-start(bf16[384,5120]{1,0:T(8,128)(2,1)} %after_ref.1) | copy-start | bytes 11796484
  29.4 13.4 %collective-permute-start.6 = (bf16[112,5120]{1,0:T(8,128)(2,1)S(1)}, bf16[112,5120]{1,0:T(8,128)(2,1)S(1)}, u32[]{:S(2)}, u32[]{:S(2)}) collective-permute-start(bf16[112,5120]{1,0:T(8,128)(2,1)S(1)} %get-tuple-element.26), channel_id=1, source_target_pairs={{0,30},{2,0},{4,2},{6,4},{8,6},{10,8},{12,10},{14,12},{16,14},{18,... | collective-permute-start | bytes 3440648 | tf_op jit(solution)/shard_map/ppermute | solution.py:21
  29.5 5.7 %collective-permute-start.3 = (bf16[224,192]{1,0:T(8,128)(2,1)S(1)}, bf16[224,192]{1,0:T(8,128)(2,1)S(1)}, u32[]{:S(2)}, u32[]{:S(2)}) collective-permute-start(bf16[224,192]{1,0:T(8,128)(2,1)S(1)} %get-tuple-element.24), channel_id=1, source_target_pairs={{0,1},{1,0},{2,3},{3,2},{4,5},{5,4},{6,7},{7,6},{8,9},{9,8},{10,11... | collective-permute-start | bytes 258056 | tf_op jit(solution)/shard_map/ppermute | solution.py:436
  31.5 17.7 %collective-permute-start.7 = (bf16[112,5120]{1,0:T(8,128)(2,1)S(1)}, bf16[112,5120]{1,0:T(8,128)(2,1)S(1)}, u32[]{:S(2)}, u32[]{:S(2)}) collective-permute-start(bf16[112,5120]{1,0:T(8,128)(2,1)S(1)} %get-tuple-element.23.prev_ref), channel_id=1, source_target_pairs={{0,1},{1,0},{4,5},{5,4},{8,9},{9,8},{12,13},{13,12},{16,17},{17,16... | collective-permute-start | bytes 3440648 | tf_op jit(solution)/shard_map/ppermute | solution.py:435
  35.3 13.9 %collective-permute-start.8 = (bf16[112,5120]{1,0:T(8,128)(2,1)S(1)}, bf16[112,5120]{1,0:T(8,128)(2,1)S(1)}, u32[]{:S(2)}, u32[]{:S(2)}) collective-permute-start(bf16[112,5120]{1,0:T(8,128)(2,1)S(1)} %stack.1.other_ref), channel_id=1, source_target_pairs={{0,2},{1,3},{4,6},{5,7},{8,10},{9,11},{12,14},{13,15},{16,18},{17,... | collective-permute-start | bytes 3440648 | tf_op jit(solution)/shard_map/ppermute | solution.py:438
  37.0 11.9 %collective-permute-start.9 = (bf16[56,5120]{1,0:T(8,128)(2,1)S(1)}, bf16[56,5120]{1,0:T(8,128)(2,1)S(1)}, u32[]{:S(2)}, u32[]{:S(2)}) collective-permute-start(bf16[56,5120]{1,0:T(8,128)(2,1)S(1)} %get-tuple-element.30), channel_id=1, source_target_pairs={{0,30},{2,0},{4,2},{6,4},{8,6},{10,8},{12,10},{14,12},{16,14},{18,... | collective-permute-start | bytes 1720328 | tf_op jit(solution)/shard_map/ppermute | solution.py:21

commit v4 on v3

--- a/solution.py
+++ b/solution.py
@@ -167,15 +167,18 @@
         return
     half = both.shape[1] // 2
 
+    low, high = both[:, :half], both[:, half:]
+    step2 = grads.shape[0]
+
     @pl.when(index_ref[0] == 0)
     def _():
-        grads_refs[0][...] = both[:, :half]
-        grads_refs[1][...] = both[:, half:]
+        grads_refs[0][...] = low
+        grads_refs[1][...] = jnp.concatenate([high[step2:], high[:step2]], axis=1)
 
     @pl.when(index_ref[0] != 0)
     def _():
-        grads_refs[0][...] = both[:, half:]
-        grads_refs[1][...] = both[:, :half]
+        grads_refs[0][...] = high
+        grads_refs[1][...] = jnp.concatenate([low[step2:], low[:step2]], axis=1)
 
     for n in range(1, n_stacks):
         for at in columns(x_ref.shape[1]):
@@ -193,7 +196,7 @@
         out_specs=[VMEM] * (2 + n_stacks + halves),
         out_shape=[pltpu.VMEM((step2, width), BF16), pltpu.VMEM((step2 // 2, width), BF16)]
         + [pltpu.VMEM((step2, width), BF16)] * n_stacks
-        + [pltpu.VMEM((2 * step2, rows // halves), BF16)] * halves,
+        + [pltpu.VMEM((2 * step2, rows // halves), BF16), pltpu.VMEM((step2, rows), BF16)][:halves],
         name="second_meeting",
         **params(6 * step2 * rows * width, 4 * rows * width),
     )(*in_vmem(x, g, grad_hidden, own_grads), index.reshape(1), *in_vmem(*weights))
@@ -329,12 +332,11 @@
 
 def ready_part_kernel(mine_ref, own_ref, prev_ref, theirs_ref, other_ref, after_ref, mine_out, theirs_out, done_ref):
     del after_ref
-    step2 = other_ref.shape[0]
     done_ref[...] = jnp.zeros_like(done_ref)
     for at in columns(own_ref.shape[1]):
         both = jnp.concatenate([own_ref[:, at], prev_ref[:, at]], axis=0)
         mine_out[:, at] = dot_left(mine_ref[...], both).astype(BF16)
-        theirs_out[:, at] = dot_left(theirs_ref[:step2, :], other_ref[:, at])
+        theirs_out[:, at] = dot_left(theirs_ref[:, theirs_out.shape[0] :], other_ref[:, at])
 
 
 def ready_part(mine, own, prev, theirs, other, after):
@@ -369,7 +371,7 @@
     del after_ref
     stores = add_rows(total_ref, own_ref, back_ref, 0, up_ref, up_sem)
     for n, at in enumerate(columns(out_ref.shape[1])):
-        term = dot_left(theirs_ref[even_ref.shape[0] :, :], even_ref[:, at] + odd_ref[:, at])
+        term = dot_left(theirs_ref[:, : out_ref.shape[0]], even_ref[:, at] + odd_ref[:, at])
         theirs = (part_ref[:, at] + term).astype(BF16)
         scratch[:, at] = (mine_ref[:, at].astype(F32) + theirs.astype(F32)).astype(BF16)
         stores.append(pltpu.make_async_copy(scratch.at[:, at], out_ref.at[:, at], sem.at[n]))

time: 52.1 us -> 52.1 us (level)
    ppermute x1, waiting for transfers between devices: 1.72 us -> 1.15 us  [local(): theirs = lax.ppermute(sent, 'tensor', swap)]
    ppermute x5, waiting for transfers between devices: 14.9 us -> 15.4 us  [from_behind(): lax.ppermute(value, axis, [(i, (i + by) % devices) for i in range(devices)])]
where the time goes in v4:
time: 52.1 us; the launch traced here: 51.9 us
  Pallas kernels  17.4 us (33%)
  waiting for transfers between devices  16.9 us (32%)
  starting transfers between devices  12.6 us (24%)
  local copies, waits for them, and re-layouts  4.24 us (8%)
  between operations  0.75 us (1%)
    ppermute x5, waiting for transfers between devices, from_behind(): lax.ppermute(value, axis, [(i, (i + by) % devices) for i in range(devices)])  15.4 us
    ppermute x5, starting transfers between devices, from_behind(): lax.ppermute(value, axis, [(i, (i + by) % devices) for i in range(devices)])  4.84 us
    pallas_call x1, Pallas kernels, own_meeting(): pl.pallas_call(own_kernel, in_specs=[VMEM] * 2 + [HBM] * 3, out_specs=[VM...  4.59 us
    unnamed x8, local copies, waits for them, and re-layouts  4.24 us
    pallas_call x1, Pallas kernels, second_meeting(): pl.pallas_call(functools.partial(second_kernel, n_stacks, halves), in_spe...  3.34 us
    pallas_call x1, Pallas kernels, last_part(): pl.pallas_call(last_kernel, in_specs=[VMEM] * 7 + [HBM], out_specs=[HBM]...  2.65 us
    pallas_call x1, Pallas kernels, totals(): pl.pallas_call(total_kernel, in_specs=[VMEM, VMEM, place], out_specs=[HBM...  2.27 us
    ppermute x1, starting transfers between devices, local(): theirs = lax.ppermute(sent, 'tensor', swap)  2.04 us
  transfers between devices with their start and end apart: 10, of which 6 were waited for; matrix products, arithmetic and copies ran while one was open for 0% of the time, Pallas kernels for 28%

profile of v4, /device:TPU:0, one launch (start us, length us, event | category | flops | bytes accessed | tf_op | source)
XLA Modules:
  0.0 51.9 jit_solution(5376761117223629484)
XLA Ops:
  0.6 0.5 collective-permute-start
  1.1 2.6 %collective-permute-start.1 = (bf16[54,5120]{1,0:T(8,128)(2,1)}, bf16[54,5120]{1,0:T(8,128)(2,1)S(1)}, u32[]{:S(2)}, u32[]{:S(2)}) collective-permute-start(bf16[54,5120]{1,0:T(8,128)(2,1)} %bitcast.14), channel_id=1, source_target_pairs={{0,2},{2,4},{4,6},{6,8},{8,10},{10,12},{12,14},{14,16},{16,18},{18... | collective-permute-start | bytes 1658888 | tf_op jit(solution)/shard_map/ppermute | solution.py:21
  3.8 0.1 collective-permute-start.2
  3.8 1.5 %collective-permute-start.4 = (bf16[54,5120]{1,0:T(8,128)(2,1)}, bf16[54,5120]{1,0:T(8,128)(2,1)S(1)}, u32[]{:S(2)}, u32[]{:S(2)}) collective-permute-start(bf16[54,5120]{1,0:T(8,128)(2,1)} %bitcast.15), channel_id=1, source_target_pairs={{0,1},{1,0},{2,3},{3,2},{4,5},{5,4},{6,7},{7,6},{8,9},{9,8},{10,11... | collective-permute-start | bytes 1658888 | tf_op jit(solution)/shard_map/ppermute | solution.py:420
  5.3 0.5 %collective-permute-start.5 = (bf16[54,5120]{1,0:T(8,128)(2,1)}, bf16[54,5120]{1,0:T(8,128)(2,1)S(1)}, u32[]{:S(2)}, u32[]{:S(2)}) collective-permute-start(bf16[54,5120]{1,0:T(8,128)(2,1)} %bitcast.18), channel_id=1, source_target_pairs={{0,1},{1,0},{2,3},{3,2},{4,5},{5,4},{6,7},{7,6},{8,9},{9,8},{10,11... | collective-permute-start | bytes 1658888 | tf_op jit(solution)/shard_map/ppermute | solution.py:420
  5.9 0.0 copy-start
  5.9 2.1 %copy-done = bf16[384,5120]{1,0:T(8,128)(2,1)S(1)} copy-done((bf16[384,5120]{1,0:T(8,128)(2,1)S(1)}, bf16[384,5120]{1,0:T(8,128)(2,1)}, u32[]{:S(2)}) %copy-start) | copy-done | bytes 3932184
  8.0 0.0 copy-start.2
  8.0 2.1 %copy-done.2 = bf16[384,5120]{1,0:T(8,128)(2,1)S(1)} copy-done((bf16[384,5120]{1,0:T(8,128)(2,1)S(1)}, bf16[384,5120]{1,0:T(8,128)(2,1)}, u32[]{:S(2)}) %copy-start.2) | copy-done | bytes 3932184
  10.1 0.0 copy-start.3
  10.1 4.6 %own_meeting.1 = (bf16[112,5120]{1,0:T(8,128)(2,1)S(1)}, bf16[112,384]{1,0:T(8,128)(2,1)S(1)}, bf16[56,384]{1,0:T(8,128)(2,1)S(1)}) custom-call(bf16[384,5120]{1,0:T(8,128)(2,1)S(1)} %copy-done, bf16[384,5120]{1,0:T(8,128)(2,1)S(1)} %copy-done.2, bf16[54,5120]{1,0:T(8,128)(2,1)} %bitcast.16, bf16[54,5120]{1,0:T(8,128)(2,1)} %bitcast.19, ...), custom_call_target="tpu_custom_call" | custom-call | flops 660602880 | bytes 7864320 | tf_op jit(solution)/shard_map/own_meeting/pallas_call | solution.py:125
  14.7 0.0 collective-permute-done.down_ref
  14.7 0.0 copy-done.3
  14.7 0.0 copy-start.1
  14.7 1.3 %grad_hidden.1.prev_ref = f32[54,384]{1,0:T(8,128)S(1)} custom-call(bf16[384,5120]{1,0:T(8,128)(2,1)S(1)} %copy-done.3, bf16[54,5120]{1,0:T(8,128)(2,1)S(1)} %collective-permute-done.down_ref, bf16[112,384]{1,0:T(8,128)(2,1)S(1)} %get-tuple-element.20.after_ref.own_ref.grads_ref), custom_call_target="tpu_custom_call" | custom-call | flops 212336640 | bytes 3932160 | tf_op jit(solution)/shard_map/grad_hidden/pallas_call | solution.py:147
  16.0 3.8 %collective-permute-done.1.refs_0_ = bf16[54,5120]{1,0:T(8,128)(2,1)S(1)} collective-permute-done((bf16[54,5120]{1,0:T(8,128)(2,1)}, bf16[54,5120]{1,0:T(8,128)(2,1)S(1)}, u32[]{:S(2)}, u32[]{:S(2)}) %collective-permute-start.1) | collective-permute-done | bytes 552992 | tf_op jit(solution)/shard_map/ppermute | solution.py:21
  19.9 6.1 %collective-permute-done.2.refs_1_ = bf16[54,5120]{1,0:T(8,128)(2,1)S(1)} collective-permute-done((bf16[54,5120]{1,0:T(8,128)(2,1)}, bf16[54,5120]{1,0:T(8,128)(2,1)S(1)}, u32[]{:S(2)}, u32[]{:S(2)}) %collective-permute-start.2) | collective-permute-done | bytes 552992 | tf_op jit(solution)/shard_map/ppermute | solution.py:21
  26.0 0.0 copy-done.1
  26.0 3.3 %second_meeting.1 = (bf16[112,5120]{1,0:T(8,128)(2,1)S(1)}, bf16[56,5120]{1,0:T(8,128)(2,1)S(1)}, bf16[112,5120]{1,0:T(8,128)(2,1)S(1)}, bf16[224,192]{1,0:T(8,128)(2,1)S(1)}, bf16[112,384]{1,0:T(8,128)(2,1)S(1)}) custom-call(bf16[384,5120]{1,0:T(8,128)(2,1)S(1)} %copy-done.1, bf16[384,5120]{1,0:T(8,128)(2,1)S(1)} %copy-done.3, ...), custom_call_target="tpu_custom_call" | custom-call | flops 1321205760 | bytes 7864320 | tf_op jit(solution)/shard_map/second_meeting/pallas_call | solution.py:193
  29.4 0.1 collective-permute-start.6
  29.4 2.0 %collective-permute-start.3 = (bf16[112,384]{1,0:T(8,128)(2,1)S(1)}, bf16[112,384]{1,0:T(8,128)(2,1)S(1)}, u32[]{:S(2)}, u32[]{:S(2)}) collective-permute-start(bf16[112,384]{1,0:T(8,128)(2,1)S(1)} %get-tuple-element.24), channel_id=1, source_target_pairs={{0,1},{1,0},{2,3},{3,2},{4,5},{5,4},{6,7},{7,6},{8,9},{9,8},{10,11... | collective-permute-start | bytes 258056 | tf_op jit(solution)/shard_map/ppermute | solution.py:438
  31.5 1.9 %collective-permute-start.7 = (bf16[112,5120]{1,0:T(8,128)(2,1)S(1)}, bf16[112,5120]{1,0:T(8,128)(2,1)S(1)}, u32[]{:S(2)}, u32[]{:S(2)}) collective-permute-start(bf16[112,5120]{1,0:T(8,128)(2,1)S(1)} %get-tuple-element.23.prev_ref), channel_id=1, source_target_pairs={{0,1},{1,0},{4,5},{5,4},{8,9},{9,8},{12,13},{13,12},{16,17},{17,16... | collective-permute-start | bytes 3440648 | tf_op jit(solution)/shard_map/ppermute | solution.py:437
  33.4 0.0 collective-permute-done.4.gate_ref
  33.4 0.0 collective-permute-done.5.up_ref
  33.5 1.1 %collective-permute-done.3.after_ref.theirs_ref = bf16[112,384]{1,0:T(8,128)(2,1)S(1)} collective-permute-done((bf16[112,384]{1,0:T(8,128)(2,1)S(1)}, bf16[112,384]{1,0:T(8,128)(2,1)S(1)}, u32[]{:S(2)}, u32[]{:S(2)}) %collective-permute-start.3) | collective-permute-done | bytes 86048 | tf_op jit(solution)/shard_map/ppermute | solution.py:438
  34.6 0.1 stack.1.other_ref
  34.7 1.8 %collective-permute-start.8 = (bf16[112,5120]{1,0:T(8,128)(2,1)S(1)}, bf16[112,5120]{1,0:T(8,128)(2,1)S(1)}, u32[]{:S(2)}, u32[]{:S(2)}) collective-permute-start(bf16[112,5120]{1,0:T(8,128)(2,1)S(1)} %stack.1.other_ref), channel_id=1, source_target_pairs={{0,2},{1,3},{4,6},{5,7},{8,10},{9,11},{12,14},{13,15},{16,18},{17,... | collective-permute-start | bytes 3440648 | tf_op jit(solution)/shard_map/ppermute | solution.py:440
  36.5 1.6 %collective-permute-start.9 = (bf16[56,5120]{1,0:T(8,128)(2,1)S(1)}, bf16[56,5120]{1,0:T(8,128)(2,1)S(1)}, u32[]{:S(2)}, u32[]{:S(2)}) collective-permute-start(bf16[56,5120]{1,0:T(8,128)(2,1)S(1)} %get-tuple-element.30), channel_id=1, source_target_pairs={{0,30},{2,0},{4,2},{6,4},{8,6},{10,8},{12,10},{14,12},{16,14},{18,... | collective-permute-start | bytes 1720328 | tf_op jit(solution)/shard_map/ppermute | solution.py:21
  38.1 4.7 %collective-permute-done.6.after_ref.back_ref = bf16[112,5120]{1,0:T(8,128)(2,1)S(1)} collective-permute-done((bf16[112,5120]{1,0:T(8,128)(2,1)S(1)}, bf16[112,5120]{1,0:T(8,128)(2,1)S(1)}, u32[]{:S(2)}, u32[]{:S(2)}) %collective-permute-start.6) | collective-permute-done | bytes 1146912 | tf_op jit(solution)/shard_map/ppermute | solution.py:21
  42.8 1.4 %own_sums.1 = (f32[112,5120]{1,0:T(8,128)S(1)}, f32[56,5120]{1,0:T(8,128)S(1)}) custom-call(bf16[384,5120]{1,0:T(8,128)(2,1)S(1)} %copy-done.1, bf16[384,5120]{1,0:T(8,128)(2,1)S(1)} %copy-done.3, bf16[56,384]{1,0:T(8,128)(2,1)S(1)} %get-tuple-element.25.hidden_ref, bf16[112,384]{1,0:T(8,128)(2,1)S(1)} %get-tuple-element.20.after_ref.own_ref.grads_ref, ...), custom_call_target="tpu_custom_call" | custom-call | flops 660602880 | bytes 7864320 | tf_op jit(solution)/shard_map/own_sums/pallas_call | solution.py:230
  44.2 2.3 %totals.1 = (f32[54,1,5120]{2,1,0:T(1,128)}, f32[54,1,5120]{2,1,0:T(1,128)}) custom-call(f32[112,5120]{1,0:T(8,128)S(1)} %get-tuple-element.31.own_ref, bf16[112,5120]{1,0:T(8,128)(2,1)S(1)} %collective-permute-done.6.after_ref.back_ref, bf16[384,5120]{1,0:T(8,128)(2,1)} %after_ref.1), custom_call_target="tpu_custom_call" | custom-call | flops 573440 | bytes 5734400 | tf_op jit(solution)/shard_map/totals/pallas_call | solution.py:259
  46.5 1.7 %ready_part.1 = (bf16[192,5120]{1,0:T(8,128)(2,1)S(1)}, f32[192,5120]{1,0:T(8,128)S(1)}, f32[8,128]{1,0:T(8,128)}) custom-call(bf16[224,192]{1,0:T(8,128)(2,1)S(1)} %get-tuple-element.21.mine_ref, bf16[112,5120]{1,0:T(8,128)(2,1)S(1)} %get-tuple-element.22.own_ref, bf16[112,5120]{1,0:T(8,128)(2,1)S(1)} %get-tuple-element.23.prev_ref, ...), custom_call_target="tpu_custom_call" | custom-call | flops 660602880 | bytes 5898240 | tf_op jit(solution)/shard_map/ready_part/pallas_call | solution.py:344
  48.2 0.7 %collective-permute-done.9.back_ref = bf16[56,5120]{1,0:T(8,128)(2,1)S(1)} collective-permute-done((bf16[56,5120]{1,0:T(8,128)(2,1)S(1)}, bf16[56,5120]{1,0:T(8,128)(2,1)S(1)}, u32[]{:S(2)}, u32[]{:S(2)}) %collective-permute-start.9) | collective-permute-done | bytes 573472 | tf_op jit(solution)/shard_map/ppermute | solution.py:21
  48.9 0.3 collective-permute-done.7.even_ref
  49.2 0.0 collective-permute-done.8.odd_ref
  49.2 2.7 %last_part.1 = (bf16[192,5120]{1,0:T(8,128)(2,1)}, f32[54,1,5120]{2,1,0:T(1,128)}) custom-call(bf16[192,5120]{1,0:T(8,128)(2,1)S(1)} %get-tuple-element.28.mine_ref, f32[192,5120]{1,0:T(8,128)S(1)} %get-tuple-element.29.part_ref, bf16[112,384]{1,0:T(8,128)(2,1)S(1)} %collective-permute-done.3.after_ref.theirs_ref, ...), custom_call_target="tpu_custom_call" | custom-call | flops 220200960 | bytes 7864320 | tf_op jit(solution)/shard_map/last_part/pallas_call | solution.py:385
Async XLA Ops:
  0.6 14.1 %collective-permute-start = (bf16[54,5120]{1,0:T(8,128)(2,1)}, bf16[54,5120]{1,0:T(8,128)(2,1)S(1)}, u32[]{:S(2)}, u32[]{:S(2)}) collective-permute-start(bf16[54,5120]{1,0:T(8,128)(2,1)} %bitcast.12), channel_id=1, source_target_pairs={{0,2},{2,4},{4,6},{6,8},{8,10},{10,12},{12,14},{14,16},{16,18},{18... | collective-permute-start | bytes 1658888 | tf_op jit(solution)/shard_map/ppermute | solution.py:21
  1.1 18.7 %collective-permute-start.1 = (bf16[54,5120]{1,0:T(8,128)(2,1)}, bf16[54,5120]{1,0:T(8,128)(2,1)S(1)}, u32[]{:S(2)}, u32[]{:S(2)}) collective-permute-start(bf16[54,5120]{1,0:T(8,128)(2,1)} %bitcast.14), channel_id=1, source_target_pairs={{0,2},{2,4},{4,6},{6,8},{8,10},{10,12},{12,14},{14,16},{16,18},{18... | collective-permute-start | bytes 1658888 | tf_op jit(solution)/shard_map/ppermute | solution.py:21
  3.8 22.3 %collective-permute-start.2 = (bf16[54,5120]{1,0:T(8,128)(2,1)}, bf16[54,5120]{1,0:T(8,128)(2,1)S(1)}, u32[]{:S(2)}, u32[]{:S(2)}) collective-permute-start(bf16[54,5120]{1,0:T(8,128)(2,1)} %bitcast.17), channel_id=1, source_target_pairs={{0,2},{2,4},{4,6},{6,8},{8,10},{10,12},{12,14},{14,16},{16,18},{18... | collective-permute-start | bytes 1658888 | tf_op jit(solution)/shard_map/ppermute | solution.py:21
  3.8 29.6 %collective-permute-start.4 = (bf16[54,5120]{1,0:T(8,128)(2,1)}, bf16[54,5120]{1,0:T(8,128)(2,1)S(1)}, u32[]{:S(2)}, u32[]{:S(2)}) collective-permute-start(bf16[54,5120]{1,0:T(8,128)(2,1)} %bitcast.15), channel_id=1, source_target_pairs={{0,1},{1,0},{2,3},{3,2},{4,5},{5,4},{6,7},{7,6},{8,9},{9,8},{10,11... | collective-permute-start | bytes 1658888 | tf_op jit(solution)/shard_map/ppermute | solution.py:420
  5.3 28.1 %collective-permute-start.5 = (bf16[54,5120]{1,0:T(8,128)(2,1)}, bf16[54,5120]{1,0:T(8,128)(2,1)S(1)}, u32[]{:S(2)}, u32[]{:S(2)}) collective-permute-start(bf16[54,5120]{1,0:T(8,128)(2,1)} %bitcast.18), channel_id=1, source_target_pairs={{0,1},{1,0},{2,3},{3,2},{4,5},{5,4},{6,7},{7,6},{8,9},{9,8},{10,11... | collective-permute-start | bytes 1658888 | tf_op jit(solution)/shard_map/ppermute | solution.py:420
  5.9 2.1 %copy-start = (bf16[384,5120]{1,0:T(8,128)(2,1)S(1)}, bf16[384,5120]{1,0:T(8,128)(2,1)}, u32[]{:S(2)}) copy-start(bf16[384,5120]{1,0:T(8,128)(2,1)} %after_ref.1) | copy-start | bytes 11796484
  8.0 2.1 %copy-start.2 = (bf16[384,5120]{1,0:T(8,128)(2,1)S(1)}, bf16[384,5120]{1,0:T(8,128)(2,1)}, u32[]{:S(2)}) copy-start(bf16[384,5120]{1,0:T(8,128)(2,1)} %g_ref.7) | copy-start | bytes 11796484
  10.1 4.6 %copy-start.3 = (bf16[384,5120]{1,0:T(8,128)(2,1)S(1)}, bf16[384,5120]{1,0:T(8,128)(2,1)}, u32[]{:S(2)}) copy-start(bf16[384,5120]{1,0:T(8,128)(2,1)} %g_ref.7) | copy-start | bytes 11796484
  14.7 11.3 %copy-start.1 = (bf16[384,5120]{1,0:T(8,128)(2,1)S(1)}, bf16[384,5120]{1,0:T(8,128)(2,1)}, u32[]{:S(2)}) copy-start(bf16[384,5120]{1,0:T(8,128)(2,1)} %after_ref.1) | copy-start | bytes 11796484
  29.4 13.4 %collective-permute-start.6 = (bf16[112,5120]{1,0:T(8,128)(2,1)S(1)}, bf16[112,5120]{1,0:T(8,128)(2,1)S(1)}, u32[]{:S(2)}, u32[]{:S(2)}) collective-permute-start(bf16[112,5120]{1,0:T(8,128)(2,1)S(1)} %get-tuple-element.26), channel_id=1, source_target_pairs={{0,30},{2,0},{4,2},{6,4},{8,6},{10,8},{12,10},{14,12},{16,14},{18,... | collective-permute-start | bytes 3440648 | tf_op jit(solution)/shard_map/ppermute | solution.py:21
  29.4 5.2 %collective-permute-start.3 = (bf16[112,384]{1,0:T(8,128)(2,1)S(1)}, bf16[112,384]{1,0:T(8,128)(2,1)S(1)}, u32[]{:S(2)}, u32[]{:S(2)}) collective-permute-start(bf16[112,384]{1,0:T(8,128)(2,1)S(1)} %get-tuple-element.24), channel_id=1, source_target_pairs={{0,1},{1,0},{2,3},{3,2},{4,5},{5,4},{6,7},{7,6},{8,9},{9,8},{10,11... | collective-permute-start | bytes 258056 | tf_op jit(solution)/shard_map/ppermute | solution.py:438
  31.5 17.7 %collective-permute-start.7 = (bf16[112,5120]{1,0:T(8,128)(2,1)S(1)}, bf16[112,5120]{1,0:T(8,128)(2,1)S(1)}, u32[]{:S(2)}, u32[]{:S(2)}) collective-permute-start(bf16[112,5120]{1,0:T(8,128)(2,1)S(1)} %get-tuple-element.23.prev_ref), channel_id=1, source_target_pairs={{0,1},{1,0},{4,5},{5,4},{8,9},{9,8},{12,13},{13,12},{16,17},{17,16... | collective-permute-start | bytes 3440648 | tf_op jit(solution)/shard_map/ppermute | solution.py:437
  34.7 14.5 %collective-permute-start.8 = (bf16[112,5120]{1,0:T(8,128)(2,1)S(1)}, bf16[112,5120]{1,0:T(8,128)(2,1)S(1)}, u32[]{:S(2)}, u32[]{:S(2)}) collective-permute-start(bf16[112,5120]{1,0:T(8,128)(2,1)S(1)} %stack.1.other_ref), channel_id=1, source_target_pairs={{0,2},{1,3},{4,6},{5,7},{8,10},{9,11},{12,14},{13,15},{16,18},{17,... | collective-permute-start | bytes 3440648 | tf_op jit(solution)/shard_map/ppermute | solution.py:440
  36.5 12.5 %collective-permute-start.9 = (bf16[56,5120]{1,0:T(8,128)(2,1)S(1)}, bf16[56,5120]{1,0:T(8,128)(2,1)S(1)}, u32[]{:S(2)}, u32[]{:S(2)}) collective-permute-start(bf16[56,5120]{1,0:T(8,128)(2,1)S(1)} %get-tuple-element.30), channel_id=1, source_target_pairs={{0,30},{2,0},{4,2},{6,4},{8,6},{10,8},{12,10},{14,12},{16,14},{18,... | collective-permute-start | bytes 1720328 | tf_op jit(solution)/shard_map/ppermute | solution.py:21

commit v5 on v3

--- a/solution.py
+++ b/solution.py
@@ -28,7 +28,7 @@
     return block
 
 
-def columns(width, limit=1280):
+def columns(width, limit=1024):
     block = column_block(width, limit)
     return [pl.ds(at, block) for at in range(0, width, block)]
 

time: 52.1 us -> 52 us (level)
  transfers between devices with their start and end apart: 10 -> 10, of which waited for: 6 -> 6; matrix products, arithmetic and copies ran while one was open for 0% -> 0% of each run, Pallas kernels for 28% -> 29%
where the time goes in v5:
time: 52 us; the launch traced here: 51.7 us
  Pallas kernels  17.5 us (34%)
  waiting for transfers between devices  16.5 us (32%)
  starting transfers between devices  12.7 us (24%)
  local copies, waits for them, and re-layouts  4.24 us (8%)
  between operations  0.75 us (1%)
    ppermute x5, waiting for transfers between devices, from_behind(): lax.ppermute(value, axis, [(i, (i + by) % devices) for i in range(devices)])  14.6 us
    ppermute x5, starting transfers between devices, from_behind(): lax.ppermute(value, axis, [(i, (i + by) % devices) for i in range(devices)])  4.88 us
    pallas_call x1, Pallas kernels, own_meeting(): pl.pallas_call(own_kernel, in_specs=[VMEM] * 2 + [HBM] * 3, out_specs=[VM...  4.58 us
    unnamed x8, local copies, waits for them, and re-layouts  4.24 us
    pallas_call x1, Pallas kernels, second_meeting(): pl.pallas_call(functools.partial(second_kernel, n_stacks, halves), in_spe...  3.32 us
    pallas_call x1, Pallas kernels, last_part(): pl.pallas_call(last_kernel, in_specs=[VMEM] * 7 + [HBM], out_specs=[HBM]...  2.57 us
    pallas_call x1, Pallas kernels, totals(): pl.pallas_call(total_kernel, in_specs=[VMEM, VMEM, place], out_specs=[HBM...  2.27 us
    ppermute x2, starting transfers between devices, local(): lax.ppermute(w, 'tensor', swap)  2.03 us
  transfers between devices with their start and end apart: 10, of which 6 were waited for; matrix products, arithmetic and copies ran while one was open for 0% of the time, Pallas kernels for 29%

profile of v5, /device:TPU:0, one launch (start us, length us, event | category | flops | bytes accessed | tf_op | source)
XLA Modules:
  0.0 51.7 jit_solution(6840963535564393369)
XLA Ops:
  0.6 0.5 collective-permute-start
  1.1 2.6 %collective-permute-start.1 = (bf16[54,5120]{1,0:T(8,128)(2,1)}, bf16[54,5120]{1,0:T(8,128)(2,1)S(1)}, u32[]{:S(2)}, u32[]{:S(2)}) collective-permute-start(bf16[54,5120]{1,0:T(8,128)(2,1)} %bitcast.14), channel_id=1, source_target_pairs={{0,2},{2,4},{4,6},{6,8},{8,10},{10,12},{12,14},{14,16},{16,18},{18... | collective-permute-start | bytes 1658888 | tf_op jit(solution)/shard_map/ppermute | solution.py:21
  3.8 0.1 collective-permute-start.2
  3.8 1.5 %collective-permute-start.4 = (bf16[54,5120]{1,0:T(8,128)(2,1)}, bf16[54,5120]{1,0:T(8,128)(2,1)S(1)}, u32[]{:S(2)}, u32[]{:S(2)}) collective-permute-start(bf16[54,5120]{1,0:T(8,128)(2,1)} %bitcast.15), channel_id=1, source_target_pairs={{0,1},{1,0},{2,3},{3,2},{4,5},{5,4},{6,7},{7,6},{8,9},{9,8},{10,11... | collective-permute-start | bytes 1658888 | tf_op jit(solution)/shard_map/ppermute | solution.py:418
  5.3 0.5 %collective-permute-start.5 = (bf16[54,5120]{1,0:T(8,128)(2,1)}, bf16[54,5120]{1,0:T(8,128)(2,1)S(1)}, u32[]{:S(2)}, u32[]{:S(2)}) collective-permute-start(bf16[54,5120]{1,0:T(8,128)(2,1)} %bitcast.18), channel_id=1, source_target_pairs={{0,1},{1,0},{2,3},{3,2},{4,5},{5,4},{6,7},{7,6},{8,9},{9,8},{10,11... | collective-permute-start | bytes 1658888 | tf_op jit(solution)/shard_map/ppermute | solution.py:418
  5.9 0.0 copy-start
  5.9 2.1 %copy-done = bf16[384,5120]{1,0:T(8,128)(2,1)S(1)} copy-done((bf16[384,5120]{1,0:T(8,128)(2,1)S(1)}, bf16[384,5120]{1,0:T(8,128)(2,1)}, u32[]{:S(2)}) %copy-start) | copy-done | bytes 3932184
  8.0 0.0 copy-start.2
  8.0 2.1 %copy-done.2 = bf16[384,5120]{1,0:T(8,128)(2,1)S(1)} copy-done((bf16[384,5120]{1,0:T(8,128)(2,1)S(1)}, bf16[384,5120]{1,0:T(8,128)(2,1)}, u32[]{:S(2)}) %copy-start.2) | copy-done | bytes 3932184
  10.1 0.0 copy-start.3
  10.1 4.6 %own_meeting.1 = (bf16[112,5120]{1,0:T(8,128)(2,1)S(1)}, bf16[112,384]{1,0:T(8,128)(2,1)S(1)}, bf16[56,384]{1,0:T(8,128)(2,1)S(1)}) custom-call(bf16[384,5120]{1,0:T(8,128)(2,1)S(1)} %copy-done, bf16[384,5120]{1,0:T(8,128)(2,1)S(1)} %copy-done.2, bf16[54,5120]{1,0:T(8,128)(2,1)} %bitcast.16, bf16[54,5120]{1,0:T(8,128)(2,1)} %bitcast.19, ...), custom_call_target="tpu_custom_call" | custom-call | flops 660602880 | bytes 7864320 | tf_op jit(solution)/shard_map/own_meeting/pallas_call | solution.py:125
  14.7 0.0 collective-permute-done.down_ref
  14.7 0.0 copy-done.3
  14.7 0.0 copy-start.1
  14.7 1.3 %grad_hidden.1.prev_ref = f32[54,384]{1,0:T(8,128)S(1)} custom-call(bf16[384,5120]{1,0:T(8,128)(2,1)S(1)} %copy-done.3, bf16[54,5120]{1,0:T(8,128)(2,1)S(1)} %collective-permute-done.down_ref, bf16[112,384]{1,0:T(8,128)(2,1)S(1)} %get-tuple-element.20.after_ref.own_ref.grads_ref), custom_call_target="tpu_custom_call" | custom-call | flops 212336640 | bytes 3932160 | tf_op jit(solution)/shard_map/grad_hidden/pallas_call | solution.py:147
  16.0 3.9 %collective-permute-done.1.refs_0_ = bf16[54,5120]{1,0:T(8,128)(2,1)S(1)} collective-permute-done((bf16[54,5120]{1,0:T(8,128)(2,1)}, bf16[54,5120]{1,0:T(8,128)(2,1)S(1)}, u32[]{:S(2)}, u32[]{:S(2)}) %collective-permute-start.1) | collective-permute-done | bytes 552992 | tf_op jit(solution)/shard_map/ppermute | solution.py:21
  19.9 6.1 %collective-permute-done.2.refs_1_ = bf16[54,5120]{1,0:T(8,128)(2,1)S(1)} collective-permute-done((bf16[54,5120]{1,0:T(8,128)(2,1)}, bf16[54,5120]{1,0:T(8,128)(2,1)S(1)}, u32[]{:S(2)}, u32[]{:S(2)}) %collective-permute-start.2) | collective-permute-done | bytes 552992 | tf_op jit(solution)/shard_map/ppermute | solution.py:21
  26.0 0.0 copy-done.1
  26.0 3.3 %second_meeting.1 = (bf16[112,5120]{1,0:T(8,128)(2,1)S(1)}, bf16[56,5120]{1,0:T(8,128)(2,1)S(1)}, bf16[112,5120]{1,0:T(8,128)(2,1)S(1)}, bf16[224,192]{1,0:T(8,128)(2,1)S(1)}, bf16[224,192]{1,0:T(8,128)(2,1)S(1)}) custom-call(bf16[384,5120]{1,0:T(8,128)(2,1)S(1)} %copy-done.1, bf16[384,5120]{1,0:T(8,128)(2,1)S(1)} %copy-done.3, ...), custom_call_target="tpu_custom_call" | custom-call | flops 1321205760 | bytes 7864320 | tf_op jit(solution)/shard_map/second_meeting/pallas_call | solution.py:190
  29.4 0.1 collective-permute-start.6
  29.4 2.0 %collective-permute-start.3 = (bf16[224,192]{1,0:T(8,128)(2,1)S(1)}, bf16[224,192]{1,0:T(8,128)(2,1)S(1)}, u32[]{:S(2)}, u32[]{:S(2)}) collective-permute-start(bf16[224,192]{1,0:T(8,128)(2,1)S(1)} %get-tuple-element.24), channel_id=1, source_target_pairs={{0,1},{1,0},{2,3},{3,2},{4,5},{5,4},{6,7},{7,6},{8,9},{9,8},{10,11... | collective-permute-start | bytes 258056 | tf_op jit(solution)/shard_map/ppermute | solution.py:436
  31.4 2.0 %collective-permute-start.7 = (bf16[112,5120]{1,0:T(8,128)(2,1)S(1)}, bf16[112,5120]{1,0:T(8,128)(2,1)S(1)}, u32[]{:S(2)}, u32[]{:S(2)}) collective-permute-start(bf16[112,5120]{1,0:T(8,128)(2,1)S(1)} %get-tuple-element.23.prev_ref), channel_id=1, source_target_pairs={{0,1},{1,0},{4,5},{5,4},{8,9},{9,8},{12,13},{13,12},{16,17},{17,16... | collective-permute-start | bytes 3440648 | tf_op jit(solution)/shard_map/ppermute | solution.py:435
  33.4 0.0 collective-permute-done.4.gate_ref
  33.4 0.0 collective-permute-done.5.up_ref
  33.4 1.7 %collective-permute-done.3.after_ref.theirs_ref = bf16[224,192]{1,0:T(8,128)(2,1)S(1)} collective-permute-done((bf16[224,192]{1,0:T(8,128)(2,1)S(1)}, bf16[224,192]{1,0:T(8,128)(2,1)S(1)}, u32[]{:S(2)}, u32[]{:S(2)}) %collective-permute-start.3) | collective-permute-done | bytes 86048 | tf_op jit(solution)/shard_map/ppermute | solution.py:436
  35.2 0.1 stack.1.other_ref
  35.2 1.8 %collective-permute-start.8 = (bf16[112,5120]{1,0:T(8,128)(2,1)S(1)}, bf16[112,5120]{1,0:T(8,128)(2,1)S(1)}, u32[]{:S(2)}, u32[]{:S(2)}) collective-permute-start(bf16[112,5120]{1,0:T(8,128)(2,1)S(1)} %stack.1.other_ref), channel_id=1, source_target_pairs={{0,2},{1,3},{4,6},{5,7},{8,10},{9,11},{12,14},{13,15},{16,18},{17,... | collective-permute-start | bytes 3440648 | tf_op jit(solution)/shard_map/ppermute | solution.py:438
  37.1 1.6 %collective-permute-start.9 = (bf16[56,5120]{1,0:T(8,128)(2,1)S(1)}, bf16[56,5120]{1,0:T(8,128)(2,1)S(1)}, u32[]{:S(2)}, u32[]{:S(2)}) collective-permute-start(bf16[56,5120]{1,0:T(8,128)(2,1)S(1)} %get-tuple-element.30), channel_id=1, source_target_pairs={{0,30},{2,0},{4,2},{6,4},{8,6},{10,8},{12,10},{14,12},{16,14},{18,... | collective-permute-start | bytes 1720328 | tf_op jit(solution)/shard_map/ppermute | solution.py:21
  38.7 4.1 %collective-permute-done.6.after_ref.back_ref = bf16[112,5120]{1,0:T(8,128)(2,1)S(1)} collective-permute-done((bf16[112,5120]{1,0:T(8,128)(2,1)S(1)}, bf16[112,5120]{1,0:T(8,128)(2,1)S(1)}, u32[]{:S(2)}, u32[]{:S(2)}) %collective-permute-start.6) | collective-permute-done | bytes 1146912 | tf_op jit(solution)/shard_map/ppermute | solution.py:21
  42.8 1.6 %own_sums.1 = (f32[112,5120]{1,0:T(8,128)S(1)}, f32[56,5120]{1,0:T(8,128)S(1)}) custom-call(bf16[384,5120]{1,0:T(8,128)(2,1)S(1)} %copy-done.1, bf16[384,5120]{1,0:T(8,128)(2,1)S(1)} %copy-done.3, bf16[56,384]{1,0:T(8,128)(2,1)S(1)} %get-tuple-element.25.hidden_ref, bf16[112,384]{1,0:T(8,128)(2,1)S(1)} %get-tuple-element.20.after_ref.own_ref.grads_ref, ...), custom_call_target="tpu_custom_call" | custom-call | flops 660602880 | bytes 7864320 | tf_op jit(solution)/shard_map/own_sums/pallas_call | solution.py:227
  44.4 2.3 %totals.1 = (f32[54,1,5120]{2,1,0:T(1,128)}, f32[54,1,5120]{2,1,0:T(1,128)}) custom-call(f32[112,5120]{1,0:T(8,128)S(1)} %get-tuple-element.31.own_ref, bf16[112,5120]{1,0:T(8,128)(2,1)S(1)} %collective-permute-done.6.after_ref.back_ref, bf16[384,5120]{1,0:T(8,128)(2,1)} %after_ref.1), custom_call_target="tpu_custom_call" | custom-call | flops 573440 | bytes 5734400 | tf_op jit(solution)/shard_map/totals/pallas_call | solution.py:256
  46.7 1.7 %ready_part.1 = (bf16[192,5120]{1,0:T(8,128)(2,1)S(1)}, f32[192,5120]{1,0:T(8,128)S(1)}, f32[8,128]{1,0:T(8,128)}) custom-call(bf16[224,192]{1,0:T(8,128)(2,1)S(1)} %get-tuple-element.21.mine_ref, bf16[112,5120]{1,0:T(8,128)(2,1)S(1)} %get-tuple-element.22.own_ref, bf16[112,5120]{1,0:T(8,128)(2,1)S(1)} %get-tuple-element.23.prev_ref, ...), custom_call_target="tpu_custom_call" | custom-call | flops 660602880 | bytes 5898240 | tf_op jit(solution)/shard_map/ready_part/pallas_call | solution.py:342
  48.4 0.5 %collective-permute-done.9.back_ref = bf16[56,5120]{1,0:T(8,128)(2,1)S(1)} collective-permute-done((bf16[56,5120]{1,0:T(8,128)(2,1)S(1)}, bf16[56,5120]{1,0:T(8,128)(2,1)S(1)}, u32[]{:S(2)}, u32[]{:S(2)}) %collective-permute-start.9) | collective-permute-done | bytes 573472 | tf_op jit(solution)/shard_map/ppermute | solution.py:21
  48.9 0.2 collective-permute-done.7.even_ref
  49.1 0.0 collective-permute-done.8.odd_ref
  49.2 2.6 %last_part.1 = (bf16[192,5120]{1,0:T(8,128)(2,1)}, f32[54,1,5120]{2,1,0:T(1,128)}) custom-call(bf16[192,5120]{1,0:T(8,128)(2,1)S(1)} %get-tuple-element.28.mine_ref, f32[192,5120]{1,0:T(8,128)S(1)} %get-tuple-element.29.part_ref, bf16[224,192]{1,0:T(8,128)(2,1)S(1)} %collective-permute-done.3.after_ref.theirs_ref, ...), custom_call_target="tpu_custom_call" | custom-call | flops 220200960 | bytes 7864320 | tf_op jit(solution)/shard_map/last_part/pallas_call | solution.py:383
Async XLA Ops:
  0.6 14.0 %collective-permute-start = (bf16[54,5120]{1,0:T(8,128)(2,1)}, bf16[54,5120]{1,0:T(8,128)(2,1)S(1)}, u32[]{:S(2)}, u32[]{:S(2)}) collective-permute-start(bf16[54,5120]{1,0:T(8,128)(2,1)} %bitcast.12), channel_id=1, source_target_pairs={{0,2},{2,4},{4,6},{6,8},{8,10},{10,12},{12,14},{14,16},{16,18},{18... | collective-permute-start | bytes 1658888 | tf_op jit(solution)/shard_map/ppermute | solution.py:21
  1.1 18.7 %collective-permute-start.1 = (bf16[54,5120]{1,0:T(8,128)(2,1)}, bf16[54,5120]{1,0:T(8,128)(2,1)S(1)}, u32[]{:S(2)}, u32[]{:S(2)}) collective-permute-start(bf16[54,5120]{1,0:T(8,128)(2,1)} %bitcast.14), channel_id=1, source_target_pairs={{0,2},{2,4},{4,6},{6,8},{8,10},{10,12},{12,14},{14,16},{16,18},{18... | collective-permute-start | bytes 1658888 | tf_op jit(solution)/shard_map/ppermute | solution.py:21
  3.8 22.3 %collective-permute-start.2 = (bf16[54,5120]{1,0:T(8,128)(2,1)}, bf16[54,5120]{1,0:T(8,128)(2,1)S(1)}, u32[]{:S(2)}, u32[]{:S(2)}) collective-permute-start(bf16[54,5120]{1,0:T(8,128)(2,1)} %bitcast.17), channel_id=1, source_target_pairs={{0,2},{2,4},{4,6},{6,8},{8,10},{10,12},{12,14},{14,16},{16,18},{18... | collective-permute-start | bytes 1658888 | tf_op jit(solution)/shard_map/ppermute | solution.py:21
  3.8 29.6 %collective-permute-start.4 = (bf16[54,5120]{1,0:T(8,128)(2,1)}, bf16[54,5120]{1,0:T(8,128)(2,1)S(1)}, u32[]{:S(2)}, u32[]{:S(2)}) collective-permute-start(bf16[54,5120]{1,0:T(8,128)(2,1)} %bitcast.15), channel_id=1, source_target_pairs={{0,1},{1,0},{2,3},{3,2},{4,5},{5,4},{6,7},{7,6},{8,9},{9,8},{10,11... | collective-permute-start | bytes 1658888 | tf_op jit(solution)/shard_map/ppermute | solution.py:418
  5.3 28.1 %collective-permute-start.5 = (bf16[54,5120]{1,0:T(8,128)(2,1)}, bf16[54,5120]{1,0:T(8,128)(2,1)S(1)}, u32[]{:S(2)}, u32[]{:S(2)}) collective-permute-start(bf16[54,5120]{1,0:T(8,128)(2,1)} %bitcast.18), channel_id=1, source_target_pairs={{0,1},{1,0},{2,3},{3,2},{4,5},{5,4},{6,7},{7,6},{8,9},{9,8},{10,11... | collective-permute-start | bytes 1658888 | tf_op jit(solution)/shard_map/ppermute | solution.py:418
  5.9 2.1 %copy-start = (bf16[384,5120]{1,0:T(8,128)(2,1)S(1)}, bf16[384,5120]{1,0:T(8,128)(2,1)}, u32[]{:S(2)}) copy-start(bf16[384,5120]{1,0:T(8,128)(2,1)} %after_ref.1) | copy-start | bytes 11796484
  8.0 2.1 %copy-start.2 = (bf16[384,5120]{1,0:T(8,128)(2,1)S(1)}, bf16[384,5120]{1,0:T(8,128)(2,1)}, u32[]{:S(2)}) copy-start(bf16[384,5120]{1,0:T(8,128)(2,1)} %g_ref.7) | copy-start | bytes 11796484
  10.1 4.6 %copy-start.3 = (bf16[384,5120]{1,0:T(8,128)(2,1)S(1)}, bf16[384,5120]{1,0:T(8,128)(2,1)}, u32[]{:S(2)}) copy-start(bf16[384,5120]{1,0:T(8,128)(2,1)} %g_ref.7) | copy-start | bytes 11796484
  14.7 11.3 %copy-start.1 = (bf16[384,5120]{1,0:T(8,128)(2,1)S(1)}, bf16[384,5120]{1,0:T(8,128)(2,1)}, u32[]{:S(2)}) copy-start(bf16[384,5120]{1,0:T(8,128)(2,1)} %after_ref.1) | copy-start | bytes 11796484
  29.4 13.4 %collective-permute-start.6 = (bf16[112,5120]{1,0:T(8,128)(2,1)S(1)}, bf16[112,5120]{1,0:T(8,128)(2,1)S(1)}, u32[]{:S(2)}, u32[]{:S(2)}) collective-permute-start(bf16[112,5120]{1,0:T(8,128)(2,1)S(1)} %get-tuple-element.26), channel_id=1, source_target_pairs={{0,30},{2,0},{4,2},{6,4},{8,6},{10,8},{12,10},{14,12},{16,14},{18,... | collective-permute-start | bytes 3440648 | tf_op jit(solution)/shard_map/ppermute | solution.py:21
  29.4 5.7 %collective-permute-start.3 = (bf16[224,192]{1,0:T(8,128)(2,1)S(1)}, bf16[224,192]{1,0:T(8,128)(2,1)S(1)}, u32[]{:S(2)}, u32[]{:S(2)}) collective-permute-start(bf16[224,192]{1,0:T(8,128)(2,1)S(1)} %get-tuple-element.24), channel_id=1, source_target_pairs={{0,1},{1,0},{2,3},{3,2},{4,5},{5,4},{6,7},{7,6},{8,9},{9,8},{10,11... | collective-permute-start | bytes 258056 | tf_op jit(solution)/shard_map/ppermute | solution.py:436
  31.4 17.7 %collective-permute-start.7 = (bf16[112,5120]{1,0:T(8,128)(2,1)S(1)}, bf16[112,5120]{1,0:T(8,128)(2,1)S(1)}, u32[]{:S(2)}, u32[]{:S(2)}) collective-permute-start(bf16[112,5120]{1,0:T(8,128)(2,1)S(1)} %get-tuple-element.23.prev_ref), channel_id=1, source_target_pairs={{0,1},{1,0},{4,5},{5,4},{8,9},{9,8},{12,13},{13,12},{16,17},{17,16... | collective-permute-start | bytes 3440648 | tf_op jit(solution)/shard_map/ppermute | solution.py:435
  35.2 13.9 %collective-permute-start.8 = (bf16[112,5120]{1,0:T(8,128)(2,1)S(1)}, bf16[112,5120]{1,0:T(8,128)(2,1)S(1)}, u32[]{:S(2)}, u32[]{:S(2)}) collective-permute-start(bf16[112,5120]{1,0:T(8,128)(2,1)S(1)} %stack.1.other_ref), channel_id=1, source_target_pairs={{0,2},{1,3},{4,6},{5,7},{8,10},{9,11},{12,14},{13,15},{16,18},{17,... | collective-permute-start | bytes 3440648 | tf_op jit(solution)/shard_map/ppermute | solution.py:438
  37.1 11.9 %collective-permute-start.9 = (bf16[56,5120]{1,0:T(8,128)(2,1)S(1)}, bf16[56,5120]{1,0:T(8,128)(2,1)S(1)}, u32[]{:S(2)}, u32[]{:S(2)}) collective-permute-start(bf16[56,5120]{1,0:T(8,128)(2,1)S(1)} %get-tuple-element.30), channel_id=1, source_target_pairs={{0,30},{2,0},{4,2},{6,4},{8,6},{10,8},{12,10},{14,12},{16,14},{18,... | collective-permute-start | bytes 1720328 | tf_op jit(solution)/shard_map/ppermute | solution.py:21

commit v6 on v3

--- a/solution.py
+++ b/solution.py
@@ -333,7 +333,7 @@
     done_ref[...] = jnp.zeros_like(done_ref)
     for at in columns(own_ref.shape[1]):
         both = jnp.concatenate([own_ref[:, at], prev_ref[:, at]], axis=0)
-        mine_out[:, at] = dot_left(mine_ref[...], both).astype(BF16)
+        mine_out[:, at] = dot_left(mine_ref[...], both).astype(BF16).astype(F32)
         theirs_out[:, at] = dot_left(theirs_ref[:step2, :], other_ref[:, at])
 
 
@@ -344,7 +344,7 @@
         in_specs=[VMEM] * 5 + [ANY],
         out_specs=[VMEM] * 3,
         out_shape=[
-            pltpu.VMEM((rows, width), BF16),
+            pltpu.VMEM((rows, width), F32),
             pltpu.VMEM((rows, width), F32),
             pltpu.VMEM((8, 128), F32),
         ],
@@ -371,7 +371,7 @@
     for n, at in enumerate(columns(out_ref.shape[1])):
         term = dot_left(theirs_ref[even_ref.shape[0] :, :], even_ref[:, at] + odd_ref[:, at])
         theirs = (part_ref[:, at] + term).astype(BF16)
-        scratch[:, at] = (mine_ref[:, at].astype(F32) + theirs.astype(F32)).astype(BF16)
+        scratch[:, at] = (mine_ref[:, at] + theirs.astype(F32)).astype(BF16)
         stores.append(pltpu.make_async_copy(scratch.at[:, at], out_ref.at[:, at], sem.at[n]))
         stores[-1].start()
     for copy in stores:

time: 52.1 us -> 52 us (level)
  no operation moved by 1% of the time
where the time goes in v6:
time: 52 us; the launch traced here: 51.8 us
  Pallas kernels  17.4 us (33%)
  waiting for transfers between devices  16.8 us (32%)
  starting transfers between devices  12.7 us (24%)
  local copies, waits for them, and re-layouts  4.24 us (8%)
  between operations  0.75 us (1%)
    ppermute x5, waiting for transfers between devices, from_behind(): lax.ppermute(value, axis, [(i, (i + by) % devices) for i in range(devices)])  14.8 us
    ppermute x5, starting transfers between devices, from_behind(): lax.ppermute(value, axis, [(i, (i + by) % devices) for i in range(devices)])  4.89 us
    pallas_call x1, Pallas kernels, own_meeting(): pl.pallas_call(own_kernel, in_specs=[VMEM] * 2 + [HBM] * 3, out_specs=[VM...  4.59 us
    unnamed x8, local copies, waits for them, and re-layouts  4.24 us
    pallas_call x1, Pallas kernels, second_meeting(): pl.pallas_call(functools.partial(second_kernel, n_stacks, halves), in_spe...  3.35 us
    pallas_call x1, Pallas kernels, last_part(): pl.pallas_call(last_kernel, in_specs=[VMEM] * 7 + [HBM], out_specs=[HBM]...  2.62 us
    pallas_call x1, Pallas kernels, totals(): pl.pallas_call(total_kernel, in_specs=[VMEM, VMEM, place], out_specs=[HBM...  2.27 us
    ppermute x2, starting transfers between devices, local(): lax.ppermute(w, 'tensor', swap)  2.03 us
  transfers between devices with their start and end apart: 10, of which 6 were waited for; matrix products, arithmetic and copies ran while one was open for 0% of the time, Pallas kernels for 28%

profile of v6, /device:TPU:0, one launch (start us, length us, event | category | flops | bytes accessed | tf_op | source)
XLA Modules:
  0.0 51.8 jit_solution(8596222784581071877)
XLA Ops:
  0.6 0.5 collective-permute-start
  1.1 2.6 %collective-permute-start.1 = (bf16[54,5120]{1,0:T(8,128)(2,1)}, bf16[54,5120]{1,0:T(8,128)(2,1)S(1)}, u32[]{:S(2)}, u32[]{:S(2)}) collective-permute-start(bf16[54,5120]{1,0:T(8,128)(2,1)} %bitcast.14), channel_id=1, source_target_pairs={{0,2},{2,4},{4,6},{6,8},{8,10},{10,12},{12,14},{14,16},{16,18},{18... | collective-permute-start | bytes 1658888 | tf_op jit(solution)/shard_map/ppermute | solution.py:21
  3.8 0.1 collective-permute-start.2
  3.8 1.5 %collective-permute-start.4 = (bf16[54,5120]{1,0:T(8,128)(2,1)}, bf16[54,5120]{1,0:T(8,128)(2,1)S(1)}, u32[]{:S(2)}, u32[]{:S(2)}) collective-permute-start(bf16[54,5120]{1,0:T(8,128)(2,1)} %bitcast.15), channel_id=1, source_target_pairs={{0,1},{1,0},{2,3},{3,2},{4,5},{5,4},{6,7},{7,6},{8,9},{9,8},{10,11... | collective-permute-start | bytes 1658888 | tf_op jit(solution)/shard_map/ppermute | solution.py:418
  5.3 0.5 %collective-permute-start.5 = (bf16[54,5120]{1,0:T(8,128)(2,1)}, bf16[54,5120]{1,0:T(8,128)(2,1)S(1)}, u32[]{:S(2)}, u32[]{:S(2)}) collective-permute-start(bf16[54,5120]{1,0:T(8,128)(2,1)} %bitcast.18), channel_id=1, source_target_pairs={{0,1},{1,0},{2,3},{3,2},{4,5},{5,4},{6,7},{7,6},{8,9},{9,8},{10,11... | collective-permute-start | bytes 1658888 | tf_op jit(solution)/shard_map/ppermute | solution.py:418
  5.9 0.0 copy-start
  5.9 2.1 %copy-done = bf16[384,5120]{1,0:T(8,128)(2,1)S(1)} copy-done((bf16[384,5120]{1,0:T(8,128)(2,1)S(1)}, bf16[384,5120]{1,0:T(8,128)(2,1)}, u32[]{:S(2)}) %copy-start) | copy-done | bytes 3932184
  8.0 0.0 copy-start.2
  8.0 2.1 %copy-done.2 = bf16[384,5120]{1,0:T(8,128)(2,1)S(1)} copy-done((bf16[384,5120]{1,0:T(8,128)(2,1)S(1)}, bf16[384,5120]{1,0:T(8,128)(2,1)}, u32[]{:S(2)}) %copy-start.2) | copy-done | bytes 3932184
  10.1 0.0 copy-start.3
  10.1 4.6 %own_meeting.1 = (bf16[112,5120]{1,0:T(8,128)(2,1)S(1)}, bf16[112,384]{1,0:T(8,128)(2,1)S(1)}, bf16[56,384]{1,0:T(8,128)(2,1)S(1)}) custom-call(bf16[384,5120]{1,0:T(8,128)(2,1)S(1)} %copy-done, bf16[384,5120]{1,0:T(8,128)(2,1)S(1)} %copy-done.2, bf16[54,5120]{1,0:T(8,128)(2,1)} %bitcast.16, bf16[54,5120]{1,0:T(8,128)(2,1)} %bitcast.19, ...), custom_call_target="tpu_custom_call" | custom-call | flops 660602880 | bytes 7864320 | tf_op jit(solution)/shard_map/own_meeting/pallas_call | solution.py:125
  14.7 0.0 collective-permute-done.down_ref
  14.7 0.0 copy-done.3
  14.7 0.0 copy-start.1
  14.7 1.3 %grad_hidden.1.prev_ref = f32[54,384]{1,0:T(8,128)S(1)} custom-call(bf16[384,5120]{1,0:T(8,128)(2,1)S(1)} %copy-done.3, bf16[54,5120]{1,0:T(8,128)(2,1)S(1)} %collective-permute-done.down_ref, bf16[112,384]{1,0:T(8,128)(2,1)S(1)} %get-tuple-element.20.after_ref.own_ref.grads_ref), custom_call_target="tpu_custom_call" | custom-call | flops 212336640 | bytes 3932160 | tf_op jit(solution)/shard_map/grad_hidden/pallas_call | solution.py:147
  16.0 3.8 %collective-permute-done.1.refs_0_ = bf16[54,5120]{1,0:T(8,128)(2,1)S(1)} collective-permute-done((bf16[54,5120]{1,0:T(8,128)(2,1)}, bf16[54,5120]{1,0:T(8,128)(2,1)S(1)}, u32[]{:S(2)}, u32[]{:S(2)}) %collective-permute-start.1) | collective-permute-done | bytes 552992 | tf_op jit(solution)/shard_map/ppermute | solution.py:21
  19.9 6.1 %collective-permute-done.2.refs_1_ = bf16[54,5120]{1,0:T(8,128)(2,1)S(1)} collective-permute-done((bf16[54,5120]{1,0:T(8,128)(2,1)}, bf16[54,5120]{1,0:T(8,128)(2,1)S(1)}, u32[]{:S(2)}, u32[]{:S(2)}) %collective-permute-start.2) | collective-permute-done | bytes 552992 | tf_op jit(solution)/shard_map/ppermute | solution.py:21
  26.0 0.0 copy-done.1
  26.0 3.3 %second_meeting.1 = (bf16[112,5120]{1,0:T(8,128)(2,1)S(1)}, bf16[56,5120]{1,0:T(8,128)(2,1)S(1)}, bf16[112,5120]{1,0:T(8,128)(2,1)S(1)}, bf16[224,192]{1,0:T(8,128)(2,1)S(1)}, bf16[224,192]{1,0:T(8,128)(2,1)S(1)}) custom-call(bf16[384,5120]{1,0:T(8,128)(2,1)S(1)} %copy-done.1, bf16[384,5120]{1,0:T(8,128)(2,1)S(1)} %copy-done.3, ...), custom_call_target="tpu_custom_call" | custom-call | flops 1321205760 | bytes 7864320 | tf_op jit(solution)/shard_map/second_meeting/pallas_call | solution.py:190
  29.4 0.1 collective-permute-start.6
  29.4 2.0 %collective-permute-start.3 = (bf16[224,192]{1,0:T(8,128)(2,1)S(1)}, bf16[224,192]{1,0:T(8,128)(2,1)S(1)}, u32[]{:S(2)}, u32[]{:S(2)}) collective-permute-start(bf16[224,192]{1,0:T(8,128)(2,1)S(1)} %get-tuple-element.24), channel_id=1, source_target_pairs={{0,1},{1,0},{2,3},{3,2},{4,5},{5,4},{6,7},{7,6},{8,9},{9,8},{10,11... | collective-permute-start | bytes 258056 | tf_op jit(solution)/shard_map/ppermute | solution.py:436
  31.5 2.0 %collective-permute-start.7 = (bf16[112,5120]{1,0:T(8,128)(2,1)S(1)}, bf16[112,5120]{1,0:T(8,128)(2,1)S(1)}, u32[]{:S(2)}, u32[]{:S(2)}) collective-permute-start(bf16[112,5120]{1,0:T(8,128)(2,1)S(1)} %get-tuple-element.23.prev_ref), channel_id=1, source_target_pairs={{0,1},{1,0},{4,5},{5,4},{8,9},{9,8},{12,13},{13,12},{16,17},{17,16... | collective-permute-start | bytes 3440648 | tf_op jit(solution)/shard_map/ppermute | solution.py:435
  33.4 0.0 collective-permute-done.4.gate_ref
  33.5 0.0 collective-permute-done.5.up_ref
  33.5 1.7 %collective-permute-done.3.after_ref.theirs_ref = bf16[224,192]{1,0:T(8,128)(2,1)S(1)} collective-permute-done((bf16[224,192]{1,0:T(8,128)(2,1)S(1)}, bf16[224,192]{1,0:T(8,128)(2,1)S(1)}, u32[]{:S(2)}, u32[]{:S(2)}) %collective-permute-start.3) | collective-permute-done | bytes 86048 | tf_op jit(solution)/shard_map/ppermute | solution.py:436
  35.2 0.1 stack.1.other_ref
  35.3 1.8 %collective-permute-start.8 = (bf16[112,5120]{1,0:T(8,128)(2,1)S(1)}, bf16[112,5120]{1,0:T(8,128)(2,1)S(1)}, u32[]{:S(2)}, u32[]{:S(2)}) collective-permute-start(bf16[112,5120]{1,0:T(8,128)(2,1)S(1)} %stack.1.other_ref), channel_id=1, source_target_pairs={{0,2},{1,3},{4,6},{5,7},{8,10},{9,11},{12,14},{13,15},{16,18},{17,... | collective-permute-start | bytes 3440648 | tf_op jit(solution)/shard_map/ppermute | solution.py:438
  37.0 1.6 %collective-permute-start.9 = (bf16[56,5120]{1,0:T(8,128)(2,1)S(1)}, bf16[56,5120]{1,0:T(8,128)(2,1)S(1)}, u32[]{:S(2)}, u32[]{:S(2)}) collective-permute-start(bf16[56,5120]{1,0:T(8,128)(2,1)S(1)} %get-tuple-element.30), channel_id=1, source_target_pairs={{0,30},{2,0},{4,2},{6,4},{8,6},{10,8},{12,10},{14,12},{16,14},{18,... | collective-permute-start | bytes 1720328 | tf_op jit(solution)/shard_map/ppermute | solution.py:21
  38.7 4.1 %collective-permute-done.6.after_ref.back_ref = bf16[112,5120]{1,0:T(8,128)(2,1)S(1)} collective-permute-done((bf16[112,5120]{1,0:T(8,128)(2,1)S(1)}, bf16[112,5120]{1,0:T(8,128)(2,1)S(1)}, u32[]{:S(2)}, u32[]{:S(2)}) %collective-permute-start.6) | collective-permute-done | bytes 1146912 | tf_op jit(solution)/shard_map/ppermute | solution.py:21
  42.8 1.4 %own_sums.1 = (f32[112,5120]{1,0:T(8,128)S(1)}, f32[56,5120]{1,0:T(8,128)S(1)}) custom-call(bf16[384,5120]{1,0:T(8,128)(2,1)S(1)} %copy-done.1, bf16[384,5120]{1,0:T(8,128)(2,1)S(1)} %copy-done.3, bf16[56,384]{1,0:T(8,128)(2,1)S(1)} %get-tuple-element.25.hidden_ref, bf16[112,384]{1,0:T(8,128)(2,1)S(1)} %get-tuple-element.20.after_ref.own_ref.grads_ref, ...), custom_call_target="tpu_custom_call" | custom-call | flops 660602880 | bytes 7864320 | tf_op jit(solution)/shard_map/own_sums/pallas_call | solution.py:227
  44.3 2.3 %totals.1 = (f32[54,1,5120]{2,1,0:T(1,128)}, f32[54,1,5120]{2,1,0:T(1,128)}) custom-call(f32[112,5120]{1,0:T(8,128)S(1)} %get-tuple-element.31.own_ref, bf16[112,5120]{1,0:T(8,128)(2,1)S(1)} %collective-permute-done.6.after_ref.back_ref, bf16[384,5120]{1,0:T(8,128)(2,1)} %after_ref.1), custom_call_target="tpu_custom_call" | custom-call | flops 573440 | bytes 5734400 | tf_op jit(solution)/shard_map/totals/pallas_call | solution.py:256
  46.5 1.7 %ready_part.1 = (f32[192,5120]{1,0:T(8,128)S(1)}, f32[192,5120]{1,0:T(8,128)S(1)}, f32[8,128]{1,0:T(8,128)}) custom-call(bf16[224,192]{1,0:T(8,128)(2,1)S(1)} %get-tuple-element.21.mine_ref, bf16[112,5120]{1,0:T(8,128)(2,1)S(1)} %get-tuple-element.22.own_ref, bf16[112,5120]{1,0:T(8,128)(2,1)S(1)} %get-tuple-element.23.prev_ref, ...), custom_call_target="tpu_custom_call" | custom-call | flops 660602880 | bytes 5898240 | tf_op jit(solution)/shard_map/ready_part/pallas_call | solution.py:342
  48.2 0.7 %collective-permute-done.9.back_ref = bf16[56,5120]{1,0:T(8,128)(2,1)S(1)} collective-permute-done((bf16[56,5120]{1,0:T(8,128)(2,1)S(1)}, bf16[56,5120]{1,0:T(8,128)(2,1)S(1)}, u32[]{:S(2)}, u32[]{:S(2)}) %collective-permute-start.9) | collective-permute-done | bytes 573472 | tf_op jit(solution)/shard_map/ppermute | solution.py:21
  49.0 0.2 collective-permute-done.7.even_ref
  49.2 0.0 collective-permute-done.8.odd_ref
  49.2 2.6 %last_part.1 = (bf16[192,5120]{1,0:T(8,128)(2,1)}, f32[54,1,5120]{2,1,0:T(1,128)}) custom-call(f32[192,5120]{1,0:T(8,128)S(1)} %get-tuple-element.28.mine_ref, f32[192,5120]{1,0:T(8,128)S(1)} %get-tuple-element.29.part_ref, bf16[224,192]{1,0:T(8,128)(2,1)S(1)} %collective-permute-done.3.after_ref.theirs_ref, ...), custom_call_target="tpu_custom_call" | custom-call | flops 220200960 | bytes 7864320 | tf_op jit(solution)/shard_map/last_part/pallas_call | solution.py:383
Async XLA Ops:
  0.6 14.1 %collective-permute-start = (bf16[54,5120]{1,0:T(8,128)(2,1)}, bf16[54,5120]{1,0:T(8,128)(2,1)S(1)}, u32[]{:S(2)}, u32[]{:S(2)}) collective-permute-start(bf16[54,5120]{1,0:T(8,128)(2,1)} %bitcast.12), channel_id=1, source_target_pairs={{0,2},{2,4},{4,6},{6,8},{8,10},{10,12},{12,14},{14,16},{16,18},{18... | collective-permute-start | bytes 1658888 | tf_op jit(solution)/shard_map/ppermute | solution.py:21
  1.1 18.7 %collective-permute-start.1 = (bf16[54,5120]{1,0:T(8,128)(2,1)}, bf16[54,5120]{1,0:T(8,128)(2,1)S(1)}, u32[]{:S(2)}, u32[]{:S(2)}) collective-permute-start(bf16[54,5120]{1,0:T(8,128)(2,1)} %bitcast.14), channel_id=1, source_target_pairs={{0,2},{2,4},{4,6},{6,8},{8,10},{10,12},{12,14},{14,16},{16,18},{18... | collective-permute-start | bytes 1658888 | tf_op jit(solution)/shard_map/ppermute | solution.py:21
  3.8 22.3 %collective-permute-start.2 = (bf16[54,5120]{1,0:T(8,128)(2,1)}, bf16[54,5120]{1,0:T(8,128)(2,1)S(1)}, u32[]{:S(2)}, u32[]{:S(2)}) collective-permute-start(bf16[54,5120]{1,0:T(8,128)(2,1)} %bitcast.17), channel_id=1, source_target_pairs={{0,2},{2,4},{4,6},{6,8},{8,10},{10,12},{12,14},{14,16},{16,18},{18... | collective-permute-start | bytes 1658888 | tf_op jit(solution)/shard_map/ppermute | solution.py:21
  3.8 29.6 %collective-permute-start.4 = (bf16[54,5120]{1,0:T(8,128)(2,1)}, bf16[54,5120]{1,0:T(8,128)(2,1)S(1)}, u32[]{:S(2)}, u32[]{:S(2)}) collective-permute-start(bf16[54,5120]{1,0:T(8,128)(2,1)} %bitcast.15), channel_id=1, source_target_pairs={{0,1},{1,0},{2,3},{3,2},{4,5},{5,4},{6,7},{7,6},{8,9},{9,8},{10,11... | collective-permute-start | bytes 1658888 | tf_op jit(solution)/shard_map/ppermute | solution.py:418
  5.3 28.1 %collective-permute-start.5 = (bf16[54,5120]{1,0:T(8,128)(2,1)}, bf16[54,5120]{1,0:T(8,128)(2,1)S(1)}, u32[]{:S(2)}, u32[]{:S(2)}) collective-permute-start(bf16[54,5120]{1,0:T(8,128)(2,1)} %bitcast.18), channel_id=1, source_target_pairs={{0,1},{1,0},{2,3},{3,2},{4,5},{5,4},{6,7},{7,6},{8,9},{9,8},{10,11... | collective-permute-start | bytes 1658888 | tf_op jit(solution)/shard_map/ppermute | solution.py:418
  5.9 2.1 %copy-start = (bf16[384,5120]{1,0:T(8,128)(2,1)S(1)}, bf16[384,5120]{1,0:T(8,128)(2,1)}, u32[]{:S(2)}) copy-start(bf16[384,5120]{1,0:T(8,128)(2,1)} %after_ref.1) | copy-start | bytes 11796484
  8.0 2.1 %copy-start.2 = (bf16[384,5120]{1,0:T(8,128)(2,1)S(1)}, bf16[384,5120]{1,0:T(8,128)(2,1)}, u32[]{:S(2)}) copy-start(bf16[384,5120]{1,0:T(8,128)(2,1)} %g_ref.7) | copy-start | bytes 11796484
  10.1 4.6 %copy-start.3 = (bf16[384,5120]{1,0:T(8,128)(2,1)S(1)}, bf16[384,5120]{1,0:T(8,128)(2,1)}, u32[]{:S(2)}) copy-start(bf16[384,5120]{1,0:T(8,128)(2,1)} %g_ref.7) | copy-start | bytes 11796484
  14.7 11.3 %copy-start.1 = (bf16[384,5120]{1,0:T(8,128)(2,1)S(1)}, bf16[384,5120]{1,0:T(8,128)(2,1)}, u32[]{:S(2)}) copy-start(bf16[384,5120]{1,0:T(8,128)(2,1)} %after_ref.1) | copy-start | bytes 11796484
  29.4 13.4 %collective-permute-start.6 = (bf16[112,5120]{1,0:T(8,128)(2,1)S(1)}, bf16[112,5120]{1,0:T(8,128)(2,1)S(1)}, u32[]{:S(2)}, u32[]{:S(2)}) collective-permute-start(bf16[112,5120]{1,0:T(8,128)(2,1)S(1)} %get-tuple-element.26), channel_id=1, source_target_pairs={{0,30},{2,0},{4,2},{6,4},{8,6},{10,8},{12,10},{14,12},{16,14},{18,... | collective-permute-start | bytes 3440648 | tf_op jit(solution)/shard_map/ppermute | solution.py:21
  29.4 5.8 %collective-permute-start.3 = (bf16[224,192]{1,0:T(8,128)(2,1)S(1)}, bf16[224,192]{1,0:T(8,128)(2,1)S(1)}, u32[]{:S(2)}, u32[]{:S(2)}) collective-permute-start(bf16[224,192]{1,0:T(8,128)(2,1)S(1)} %get-tuple-element.24), channel_id=1, source_target_pairs={{0,1},{1,0},{2,3},{3,2},{4,5},{5,4},{6,7},{7,6},{8,9},{9,8},{10,11... | collective-permute-start | bytes 258056 | tf_op jit(solution)/shard_map/ppermute | solution.py:436
  31.5 17.7 %collective-permute-start.7 = (bf16[112,5120]{1,0:T(8,128)(2,1)S(1)}, bf16[112,5120]{1,0:T(8,128)(2,1)S(1)}, u32[]{:S(2)}, u32[]{:S(2)}) collective-permute-start(bf16[112,5120]{1,0:T(8,128)(2,1)S(1)} %get-tuple-element.23.prev_ref), channel_id=1, source_target_pairs={{0,1},{1,0},{4,5},{5,4},{8,9},{9,8},{12,13},{13,12},{16,17},{17,16... | collective-permute-start | bytes 3440648 | tf_op jit(solution)/shard_map/ppermute | solution.py:435
  35.3 13.9 %collective-permute-start.8 = (bf16[112,5120]{1,0:T(8,128)(2,1)S(1)}, bf16[112,5120]{1,0:T(8,128)(2,1)S(1)}, u32[]{:S(2)}, u32[]{:S(2)}) collective-permute-start(bf16[112,5120]{1,0:T(8,128)(2,1)S(1)} %stack.1.other_ref), channel_id=1, source_target_pairs={{0,2},{1,3},{4,6},{5,7},{8,10},{9,11},{12,14},{13,15},{16,18},{17,... | collective-permute-start | bytes 3440648 | tf_op jit(solution)/shard_map/ppermute | solution.py:438
  37.0 11.9 %collective-permute-start.9 = (bf16[56,5120]{1,0:T(8,128)(2,1)S(1)}, bf16[56,5120]{1,0:T(8,128)(2,1)S(1)}, u32[]{:S(2)}, u32[]{:S(2)}) collective-permute-start(bf16[56,5120]{1,0:T(8,128)(2,1)S(1)} %get-tuple-element.30), channel_id=1, source_target_pairs={{0,30},{2,0},{4,2},{6,4},{8,6},{10,8},{12,10},{14,12},{16,14},{18,... | collective-permute-start | bytes 1720328 | tf_op jit(solution)/shard_map/ppermute | solution.py:21
